TPU v7x, 32 devices: a whole 2x2x4 slice. The times are simulated.
32 devices in a mesh: gx: 4 (over y, core), gy: 8 (over z, x).
Axes of the slice: x: 2, y: 2, z: 4, core: 2. Of those that a mesh axis runs over, the one named last changes fastest.
Arguments:
- multipoles: float32 [81, 16384], P(None, ('gx', 'gy')), may hold values from -6 to 6
- parent_locals: float32 [81, 2048], P(None, ('gx', 'gy')), may hold values from -6 to 6
- m2l_ops: float32 [81, 81, 256], replicated, may hold values from -0.0625 to 0.0625
- l2l_ops: float32 [8, 81, 81], replicated, may hold values from -0.625 to 0.625
- export_cells: int32 [32, 26, 128], P(('gx', 'gy')), may hold values from 0 to 511
- pair_first: int32 [32, 256, 64], P(('gx', 'gy')), may hold values from 0 to 511
- pair_second: int32 [32, 256, 64], P(('gx', 'gy')), may hold values from 0 to 3839, as said below
- pair_count: int32 [32, 256], P(('gx', 'gy')), may hold values from 32 to 64, as said below
- parent_of: int32 [16384], P(('gx', 'gy')), may hold values from 0 to 2047, as said below
- octant: int32 [16384], P(('gx', 'gy')), may hold values from 0 to 7
Outputs:
- local_expansions: float32 [81, 16384], P(None, ('gx', 'gy'))
Inputs may be any that keep to these rules, and one draw needn't show every extreme that they name: `pair_count`: every segment has a translation vector whose 64 slots are all live. `parent_of`: the parent of a cell of segment d lies among parents d * 64 - 16 to (d + 1) * 64 + 15; every segment's first cell takes the lowest of these that exists and its last cell the highest. `pair_second`: a value of 512 or more always names a peer segment that exists.
All inputs are finite; a program needn't handle non-finite values.
Results may differ from a plain program's by a relative error of at most 0.0003.
Values sent between devices are 32-bit elements; how exact they have to be, the bound alone decides.
No kernel may reach another device: no remote copies, remote signals or barrier semaphores. Data moves between devices by JAX's collectives and lax.ppermute only.
A program may use at most 128 MiB of HBM per device.

v0:
```python
import jax
import jax.numpy as jnp
from jax import lax
from jax.sharding import PartitionSpec as P

ORDER = 8
HALO = 16


def shifted(block, axis, distance):
    devices = range(lax.axis_size(axis))
    route = [(i - distance, i) for i in devices if i - distance in devices]
    return lax.ppermute(block, axis, route)


def padded_2(shard, sides, width):
    for axis, dim in sides:
        size, length = (lax.axis_size(axis), shard.shape[dim])
        up = [(i, (i + 1) % size) for i in range(size - 1)]
        down = [(j, i) for i, j in up]
        last = lax.slice_in_dim(shard, length - width, length, axis=dim)
        first = lax.slice_in_dim(shard, 0, width, axis=dim)
        before = lax.ppermute(last, axis, up)
        after = lax.ppermute(first, axis, down)
        shard = jnp.concatenate([before, shard, after], axis=dim)
    return shard


def parity(coeff_count):
    coeff_index = jnp.arange(coeff_count, dtype=jnp.int32)
    degree = jnp.zeros((coeff_count,), jnp.int32)
    for degree_step in range(1, ORDER + 1):
        degree = degree + (coeff_index >= degree_step * degree_step).astype(jnp.int32)
    return (1 - 2 * (degree % 2)).astype(jnp.float32)


def peer_offset(peer_slot, reach):
    return peer_slot - reach if peer_slot < reach else peer_slot - reach + 1


def shards(
    multipoles,
    parent_locals,
    m2l_ops,
    l2l_ops,
    export_cells,
    pair_first,
    pair_second,
    pair_count,
    parent_of,
    octant,
):
    coeffs, cell_count = multipoles.shape
    peer_total = export_cells.shape[1]
    reach = peer_total // 2
    send_width = export_cells.shape[2]
    classes = m2l_ops.shape[2]
    slot_count = pair_first.shape[2]
    parity_sign = parity(coeffs)
    owner_index = lax.axis_index("gx") * lax.axis_size("gy") + lax.axis_index("gy")
    exported = export_cells[0].reshape(-1)
    outgoing = multipoles[:, exported].reshape(coeffs, peer_total, send_width)
    received = [
        shifted(outgoing[:, peer_slot], ("gx", "gy"), peer_offset(peer_slot, reach))
        for peer_slot in range(peer_total)
    ]
    arrived = jnp.stack(received[::-1], axis=1)
    extended = jnp.concatenate(
        [multipoles, arrived.reshape(coeffs, peer_total * send_width)], axis=1
    )
    near_local = jnp.zeros((coeffs, cell_count), jnp.float32)
    outbound = jnp.zeros_like(extended)
    class_block = classes // 4
    slot_line = lax.broadcasted_iota(jnp.int32, (class_block, slot_count), 1)
    for quarter in range(4):
        start_class = quarter * class_block
        target_cell = pair_first[0, start_class : start_class + class_block]
        source_cell = pair_second[0, start_class : start_class + class_block]
        live_mask = (
            slot_line < pair_count[0, start_class : start_class + class_block][:, None]
        ).astype(jnp.float32)
        columns = jnp.concatenate(
            [extended[:, source_cell], multipoles[:, target_cell] * parity_sign[:, None, None]],
            axis=2,
        )
        product = jnp.einsum(
            "ijk,jkq->ikq",
            m2l_ops[:, :, start_class : start_class + class_block],
            columns,
            precision=lax.Precision.HIGHEST,
        )
        near_local = near_local.at[:, target_cell].add(product[:, :, :slot_count] * live_mask)
        outbound = outbound.at[:, source_cell].add(
            product[:, :, slot_count:] * (live_mask * parity_sign[:, None, None])
        )
    returned = outbound[:, cell_count:].reshape(coeffs, peer_total, send_width)
    received_back = [
        shifted(returned[:, peer_slot], ("gx", "gy"), peer_offset(peer_slot, reach))
        for peer_slot in range(peer_total)
    ]
    arrived_back = jnp.stack(received_back[::-1], axis=1)
    near_local = near_local + outbound[:, :cell_count]
    near_local = near_local.at[:, exported].add(
        arrived_back.reshape(coeffs, peer_total * send_width)
    )
    padded = padded_2(parent_locals, ((("gx", "gy"), 1),), HALO)
    position = parent_of - owner_index * parent_locals.shape[1] + HALO
    gathered = padded[:, position]
    from_parent = jnp.zeros((coeffs, cell_count), jnp.float32)
    for child_octant in range(8):
        octant_term = jnp.dot(
            l2l_ops[child_octant],
            gathered,
            precision=lax.Precision.HIGHEST,
            preferred_element_type=jnp.float32,
        )
        from_parent = from_parent + jnp.where((octant == child_octant)[None, :], octant_term, 0.0)
    return from_parent + near_local


def solution(mesh):
    placed = (
        P(None, ("gx", "gy")),
        P(None, ("gx", "gy")),
        P(),
        P(),
        P(("gx", "gy"), None, None),
        P(("gx", "gy"), None, None),
        P(("gx", "gy"), None, None),
        P(("gx", "gy"), None),
        P(("gx", "gy")),
        P(("gx", "gy")),
    )
    return jax.shard_map(
        shards, mesh=mesh, in_specs=placed, out_specs=P(None, ("gx", "gy")), check_vma=False
    )
```

profile of v0, /device:TPU:0, one launch (start us, length us, event | category | flops | bytes accessed | tf_op | source)
XLA Modules:
  0.0 663.0 jit_solution(6609713007180011230)
XLA Ops:
  28.1 10.8 %gather_fusion.9 = f32[4096,81]{1,0:T(8,128)S(1)} fusion(f32[81,512]{0,1:T(8,128)S(1)} %copy.134, s32[4096]{0:T(1024)S(1)} %get-tuple-element.108), kind=kCustom, calls=%fused_computation.9 | custom fusion | bytes 2670592 | tf_op jit(solution)/shard_map/gather | solution.py:83
  39.2 14.2 %gather_fusion.5 = f32[4096,81]{1,0:T(8,128)} fusion(f32[81,512]{0,1:T(8,128)S(1)} %copy.134, s32[4096]{0:T(1024)S(1)} %get-tuple-element.110), kind=kCustom, calls=%fused_computation.5 | custom fusion | bytes 2670592 | tf_op jit(solution)/shard_map/gather | solution.py:83
  53.4 14.2 %gather_fusion.7 = f32[4096,81]{1,0:T(8,128)} fusion(f32[81,512]{0,1:T(8,128)S(1)} %copy.134, s32[4096]{0:T(1024)S(1)} %get-tuple-element.109), kind=kCustom, calls=%fused_computation.7 | custom fusion | bytes 2670592 | tf_op jit(solution)/shard_map/gather | solution.py:83
  67.7 14.2 %gather_fusion.3 = f32[4096,81]{1,0:T(8,128)} fusion(f32[81,512]{0,1:T(8,128)S(1)} %copy.134, s32[4096]{0:T(1024)S(1)} %broadcast_clamp_fusion.7), kind=kCustom, calls=%fused_computation.3 | custom fusion | bytes 2670592 | tf_op jit(solution)/shard_map/gather | solution.py:83
  81.9 12.5 %fusion.75 = (f32[81,81,64]{2,1,0:T(8,128)}, f32[81,81,64]{2,1,0:T(8,128)}, f32[81,81,64]{2,1,0:T(8,128)}, f32[81,81,64]{2,1,0:T(8,128)}) fusion(f32[81,81,256]{2,1,0:T(8,128)} %param.12), kind=kLoop, calls=%fused_computation.215 | loop fusion | bytes 13436928 | tf_op jit(solution)/shard_map/slice | solution.py:88
  195.3 14.2 %gather_fusion.6 = f32[4096,81]{1,0:T(8,128)} fusion(f32[81,3840]{0,1:T(8,128)S(1)} %pad_maximum_fusion, s32[4096]{0:T(1024)S(1)} %get-tuple-element.105), kind=kCustom, calls=%fused_computation.6 | custom fusion | bytes 2670592 | tf_op jit(solution)/shard_map/gather | solution.py:83
  209.5 10.6 %fusion.27 = f32[81,64,128]{2,0,1:T(8,128)S(1)} fusion(f32[81,81,64]{1,0,2:T(8,128)} %copy.206, f32[81,64,64]{0,2,1:T(8,128)} %get-tuple-element.101, f32[81,64,64]{0,2,1:T(8,128)} %bitcast.283), kind=kOutput, calls=%fused_computation.57 | convolution fusion | flops 645636096 | bytes 6988032 | tf_op jit(solution)/shard_map/ijk,jkq->ikq/dot_general | solution.py:86
  226.9 14.2 %gather_fusion.4 = f32[4096,81]{1,0:T(8,128)} fusion(f32[81,3840]{0,1:T(8,128)S(1)} %pad_maximum_fusion, s32[4096]{0:T(1024)S(1)} %get-tuple-element.106), kind=kCustom, calls=%fused_computation.4 | custom fusion | bytes 2670592 | tf_op jit(solution)/shard_map/gather | solution.py:83
  241.1 10.6 %fusion.30 = f32[81,64,128]{2,0,1:T(8,128)S(1)} fusion(f32[81,81,64]{1,0,2:T(8,128)} %copy.205, f32[81,64,64]{0,2,1:T(8,128)} %get-tuple-element.100, f32[81,64,64]{0,2,1:T(8,128)} %bitcast.284), kind=kOutput, calls=%fused_computation.58 | convolution fusion | flops 645636096 | bytes 6988032 | tf_op jit(solution)/shard_map/ijk,jkq->ikq/dot_general | solution.py:86
  258.6 14.2 %gather_fusion.2 = f32[4096,81]{1,0:T(8,128)} fusion(f32[81,3840]{0,1:T(8,128)S(1)} %pad_maximum_fusion, s32[4096]{0:T(1024)S(1)} %get-tuple-element.107), kind=kCustom, calls=%fused_computation.2 | custom fusion | bytes 2670592 | tf_op jit(solution)/shard_map/gather | solution.py:83
  272.8 11.0 %fusion.33 = f32[81,64,128]{2,0,1:T(8,128)S(1)} fusion(f32[81,81,64]{1,0,2:T(8,128)} %copy.204, f32[81,64,64]{0,2,1:T(8,128)} %get-tuple-element.102, f32[81,64,64]{0,2,1:T(8,128)} %bitcast.285), kind=kOutput, calls=%fused_computation.59 | convolution fusion | flops 645636096 | bytes 6988032 | tf_op jit(solution)/shard_map/ijk,jkq->ikq/dot_general | solution.py:86
  290.7 14.2 %gather_fusion.8 = f32[4096,81]{1,0:T(8,128)} fusion(f32[81,3840]{0,1:T(8,128)S(1)} %pad_maximum_fusion, s32[4096]{0:T(1024)S(1)} %get-tuple-element.104), kind=kCustom, calls=%fused_computation.8 | custom fusion | bytes 2670592 | tf_op jit(solution)/shard_map/gather | solution.py:83
  304.9 10.6 %fusion.24 = f32[81,64,128]{2,0,1:T(8,128)S(1)} fusion(f32[81,81,64]{1,0,2:T(8,128)} %copy.207, f32[81,64,64]{0,2,1:T(8,128)} %get-tuple-element.99, f32[81,64,64]{0,2,1:T(8,128)} %bitcast.282), kind=kOutput, calls=%fused_computation.56 | convolution fusion | flops 645636096 | bytes 6988032 | tf_op jit(solution)/shard_map/ijk,jkq->ikq/dot_general | solution.py:86
  320.3 23.1 %scatter_custom_fusion = f32[81,3840]{0,1:T(8,128)S(1)} fusion(s32[4096]{0:T(1024)S(1)} %reshape.477, f32[4096,81]{1,0:T(8,128)} %bitcast.299, f32[]{:T(128)} %constant.28.clone.1), kind=kCustom, calls=%fused_computation.77 | custom fusion | flops 331776 | bytes 1244672 | tf_op jit(solution)/shard_map/scatter-add | solution.py:93
  343.5 23.6 %scatter_fusion = f32[81,3840]{0,1:T(8,128)S(1)} fusion(f32[81,3840]{0,1:T(8,128)S(1)} %scatter_custom_fusion, s32[4096]{0:T(1024)S(1)} %reshape.485, f32[4096,81]{1,0:T(8,128)} %bitcast.287), kind=kCustom, calls=%fused_computation.11 | custom fusion | flops 331776 | bytes 3997696 | tf_op jit(solution)/shard_map/scatter-add | solution.py:93
  367.1 23.4 %scatter_fusion.1 = f32[81,3840]{0,1:T(8,128)S(1)} fusion(f32[81,3840]{0,1:T(8,128)S(1)} %scatter_fusion, s32[4096]{0:T(1024)S(1)} %reshape.493, f32[4096,81]{1,0:T(8,128)} %bitcast.286), kind=kCustom, calls=%fused_computation.12 | custom fusion | flops 331776 | bytes 3997696 | tf_op jit(solution)/shard_map/scatter-add | solution.py:93
  390.5 23.4 %scatter_fusion.2 = f32[81,3840]{0,1:T(8,128)S(1)} fusion(f32[81,3840]{0,1:T(8,128)S(1)} %scatter_fusion.1, s32[4096]{0:T(1024)S(1)} %reshape.501, f32[4096,81]{1,0:T(8,128)} %bitcast.289), kind=kCustom, calls=%fused_computation.13 | custom fusion | flops 331776 | bytes 3997696 | tf_op jit(solution)/shard_map/scatter-add | solution.py:93
  416.7 10.2 %collective-permute-start.35 = (f32[81,128]{1,0:T(8,128)}, f32[81,128]{1,0:T(8,128)}, u32[]{:S(2)}, u32[]{:S(2)}) collective-permute-start(f32[81,128]{1,0:T(8,128)} %bitcast.122), channel_id=1, source_target_pairs={{0,6},{1,7},{2,8},{3,9},{4,10},{5,11},{6,12},{7,13},{8,14},{9,15},... | collective-permute-start | bytes 124424 | tf_op jit(solution)/shard_map/ppermute | solution.py:13
  479.1 12.4 %collective-permute-start.28 = (f32[81,128]{1,0:T(8,128)S(1)}, f32[81,128]{1,0:T(8,128)S(1)}, u32[]{:S(2)}, u32[]{:S(2)}) collective-permute-start(f32[81,128]{1,0:T(8,128)S(1)} %bitcast.310), channel_id=1, source_target_pairs={{0,13},{1,14},{2,15},{3,16},{4,17},{5,18},{6,19},{7,20},{8,21},{9,... | collective-permute-start | bytes 124424 | tf_op jit(solution)/shard_map/ppermute | solution.py:13
  526.0 23.0 %scatter_fusion.3 = f32[81,512]{0,1:T(8,128)S(1)} fusion(f32[81,512]{0,1:T(8,128)S(1)} %copy.160, s32[4096]{0:T(1024)S(1)} %reshape.421, f32[4096,81]{1,0:T(8,128)} %bitcast.291), kind=kCustom, calls=%fused_computation.14 | custom fusion | flops 331776 | bytes 3997696 | tf_op jit(solution)/shard_map/scatter-add | solution.py:92
  549.0 22.8 %scatter_fusion.4 = f32[81,512]{0,1:T(8,128)S(1)} fusion(f32[81,512]{0,1:T(8,128)S(1)} %scatter_fusion.3, s32[4096]{0:T(1024)S(1)} %copy-done.7, f32[4096,81]{1,0:T(8,128)} %bitcast.292), kind=kCustom, calls=%fused_computation.15 | custom fusion | flops 331776 | bytes 3997696 | tf_op jit(solution)/shard_map/scatter-add | solution.py:92
  571.8 22.8 %scatter_fusion.5 = f32[81,512]{0,1:T(8,128)S(1)} fusion(f32[81,512]{0,1:T(8,128)S(1)} %scatter_fusion.4, s32[4096]{0:T(1024)S(1)} %copy-done.9, f32[4096,81]{1,0:T(8,128)} %bitcast.290), kind=kCustom, calls=%fused_computation.16 | custom fusion | flops 331776 | bytes 3997696 | tf_op jit(solution)/shard_map/scatter-add | solution.py:92
  594.6 22.5 %scatter_fusion.6 = f32[81,512]{0,1:T(8,128)S(1)} fusion(f32[81,512]{0,1:T(8,128)S(1)} %scatter_fusion.5, s32[4096]{0:T(1024)S(1)} %copy-done.5, f32[4096,81]{1,0:T(8,128)S(1)} %bitcast.288), kind=kCustom, calls=%fused_computation.17 | custom fusion | flops 331776 | bytes 3997696 | tf_op jit(solution)/shard_map/scatter-add | solution.py:92
  641.7 20.0 %scatter_fusion.7 = f32[81,512]{0,1:T(8,128)S(1)} fusion(f32[81,512]{0,1:T(8,128)S(1)} %scatter_fusion.6, s32[3328]{0:T(1024)S(1)} %copy-done.14, f32[3328,81]{1,0:T(8,128)S(1)} %copy.190), kind=kCustom, calls=%fused_computation.18 | custom fusion | flops 269568 | bytes 3248128 | tf_op jit(solution)/shard_map/scatter-add | solution.py:103
  (364 shorter events, 268.1 us)
Async XLA Ops:
  9.2 125.3 %collective-permute-start.2 = (f32[81,128]{0,1:T(8,128)}, f32[81,128]{0,1:T(8,128)}, u32[]{:S(2)}, u32[]{:S(2)}) collective-permute-start(f32[81,128]{0,1:T(8,128)} %get-tuple-element.68), channel_id=1, source_target_pairs={{0,13},{1,14},{2,15},{3,16},{4,17},{5,18},{6,19},{7,20},{8,21},{9,... | collective-permute-start | bytes 124424 | tf_op jit(solution)/shard_map/ppermute | solution.py:13
  16.1 121.9 %collective-permute-start.3 = (f32[81,128]{0,1:T(8,128)}, f32[81,128]{0,1:T(8,128)}, u32[]{:S(2)}, u32[]{:S(2)}) collective-permute-start(f32[81,128]{0,1:T(8,128)} %get-tuple-element.67), channel_id=1, source_target_pairs={{0,12},{1,13},{2,14},{3,15},{4,16},{5,17},{6,18},{7,19},{8,20},{9,... | collective-permute-start | bytes 124424 | tf_op jit(solution)/shard_map/ppermute | solution.py:13
  19.6 125.7 %collective-permute-start.4 = (f32[81,128]{0,1:T(8,128)}, f32[81,128]{0,1:T(8,128)}, u32[]{:S(2)}, u32[]{:S(2)}) collective-permute-start(f32[81,128]{0,1:T(8,128)} %get-tuple-element.66), channel_id=1, source_target_pairs={{0,11},{1,12},{2,13},{3,14},{4,15},{5,16},{6,17},{7,18},{8,19},{9,... | collective-permute-start | bytes 124424 | tf_op jit(solution)/shard_map/ppermute | solution.py:13
  22.8 103.1 %collective-permute-start = (f32[81,16]{0,1:T(8,128)S(1)}, f32[81,16]{0,1:T(8,128)S(1)}, u32[]{:S(2)}, u32[]{:S(2)}) collective-permute-start(f32[81,16]{0,1:T(8,128)S(1)} %get-tuple-element.85), channel_id=1, source_target_pairs={{0,1},{1,2},{2,3},{3,4},{4,5},{5,6},{6,7},{7,8},{8,9},{9,10},{10,1... | collective-permute-start | bytes 15560 | tf_op jit(solution)/shard_map/ppermute | solution.py:23
  25.0 105.6 %collective-permute-start.1 = (f32[81,16]{0,1:T(8,128)S(1)}, f32[81,16]{0,1:T(8,128)S(1)}, u32[]{:S(2)}, u32[]{:S(2)}) collective-permute-start(f32[81,16]{0,1:T(8,128)S(1)} %get-tuple-element.86), channel_id=1, source_target_pairs={{1,0},{2,1},{3,2},{4,3},{5,4},{6,5},{7,6},{8,7},{9,8},{10,9},{11,1... | collective-permute-start | bytes 15560 | tf_op jit(solution)/shard_map/ppermute | solution.py:24
  125.8 21.7 %collective-permute-start.5 = (f32[81,128]{0,1:T(8,128)}, f32[81,128]{0,1:T(8,128)S(1)}, u32[]{:S(2)}, u32[]{:S(2)}) collective-permute-start(f32[81,128]{0,1:T(8,128)} %get-tuple-element.65), channel_id=1, source_target_pairs={{0,10},{1,11},{2,12},{3,13},{4,14},{5,15},{6,16},{7,17},{8,18},{9,... | collective-permute-start | bytes 124424 | tf_op jit(solution)/shard_map/ppermute | solution.py:13
  130.6 18.3 %collective-permute-start.6 = (f32[81,128]{0,1:T(8,128)}, f32[81,128]{0,1:T(8,128)S(1)}, u32[]{:S(2)}, u32[]{:S(2)}) collective-permute-start(f32[81,128]{0,1:T(8,128)} %get-tuple-element.64), channel_id=1, source_target_pairs={{0,9},{1,10},{2,11},{3,12},{4,13},{5,14},{6,15},{7,16},{8,17},{9,1... | collective-permute-start | bytes 124424 | tf_op jit(solution)/shard_map/ppermute | solution.py:13
  134.5 17.5 %collective-permute-start.7 = (f32[81,128]{0,1:T(8,128)S(1)}, f32[81,128]{0,1:T(8,128)S(1)}, u32[]{:S(2)}, u32[]{:S(2)}) collective-permute-start(f32[81,128]{0,1:T(8,128)S(1)} %copy-done.18), channel_id=1, source_target_pairs={{0,8},{1,9},{2,10},{3,11},{4,12},{5,13},{6,14},{7,15},{8,16},{9,17... | collective-permute-start | bytes 124424 | tf_op jit(solution)/shard_map/ppermute | solution.py:13
  138.0 16.6 %collective-permute-start.8 = (f32[81,128]{0,1:T(8,128)S(1)}, f32[81,128]{0,1:T(8,128)S(1)}, u32[]{:S(2)}, u32[]{:S(2)}) collective-permute-start(f32[81,128]{0,1:T(8,128)S(1)} %copy-done.17), channel_id=1, source_target_pairs={{0,7},{1,8},{2,9},{3,10},{4,11},{5,12},{6,13},{7,14},{8,15},{9,16}... | collective-permute-start | bytes 124424 | tf_op jit(solution)/shard_map/ppermute | solution.py:13
  416.7 28.2 %collective-permute-start.35 = (f32[81,128]{1,0:T(8,128)}, f32[81,128]{1,0:T(8,128)}, u32[]{:S(2)}, u32[]{:S(2)}) collective-permute-start(f32[81,128]{1,0:T(8,128)} %bitcast.122), channel_id=1, source_target_pairs={{0,6},{1,7},{2,8},{3,9},{4,10},{5,11},{6,12},{7,13},{8,14},{9,15},... | collective-permute-start | bytes 124424 | tf_op jit(solution)/shard_map/ppermute | solution.py:13
  428.8 23.1 %collective-permute-start.36 = (f32[81,128]{1,0:T(8,128)}, f32[81,128]{1,0:T(8,128)}, u32[]{:S(2)}, u32[]{:S(2)}) collective-permute-start(f32[81,128]{1,0:T(8,128)} %bitcast.123), channel_id=1, source_target_pairs={{0,5},{1,6},{2,7},{3,8},{4,9},{5,10},{6,11},{7,12},{8,13},{9,14},{... | collective-permute-start | bytes 124424 | tf_op jit(solution)/shard_map/ppermute | solution.py:13
  432.3 21.0 %collective-permute-start.37 = (f32[81,128]{1,0:T(8,128)}, f32[81,128]{1,0:T(8,128)}, u32[]{:S(2)}, u32[]{:S(2)}) collective-permute-start(f32[81,128]{1,0:T(8,128)} %bitcast.124), channel_id=1, source_target_pairs={{0,4},{1,5},{2,6},{3,7},{4,8},{5,9},{6,10},{7,11},{8,12},{9,13},{1... | collective-permute-start | bytes 124424 | tf_op jit(solution)/shard_map/ppermute | solution.py:13
  437.7 16.9 %collective-permute-start.38 = (f32[81,128]{1,0:T(8,128)}, f32[81,128]{1,0:T(8,128)}, u32[]{:S(2)}, u32[]{:S(2)}) collective-permute-start(f32[81,128]{1,0:T(8,128)} %bitcast.125), channel_id=1, source_target_pairs={{0,3},{1,4},{2,5},{3,6},{4,7},{5,8},{6,9},{7,10},{8,11},{9,12},{10... | collective-permute-start | bytes 124424 | tf_op jit(solution)/shard_map/ppermute | solution.py:13
  469.3 22.2 %collective-permute-start.50 = (f32[81,128]{1,0:T(8,128)S(1)}, f32[81,128]{1,0:T(8,128)S(1)}, u32[]{:S(2)}, u32[]{:S(2)}) collective-permute-start(f32[81,128]{1,0:T(8,128)S(1)} %bitcast.306), channel_id=1, source_target_pairs={{10,0},{11,1},{12,2},{13,3},{14,4},{15,5},{16,6},{17,7},{18,8},{19... | collective-permute-start | bytes 124424 | tf_op jit(solution)/shard_map/ppermute | solution.py:13
  474.0 26.7 %collective-permute-start.51 = (f32[81,128]{1,0:T(8,128)}, f32[81,128]{1,0:T(8,128)}, u32[]{:S(2)}, u32[]{:S(2)}) collective-permute-start(f32[81,128]{1,0:T(8,128)} %bitcast.138), channel_id=1, source_target_pairs={{11,0},{12,1},{13,2},{14,3},{15,4},{16,5},{17,6},{18,7},{19,8},{20... | collective-permute-start | bytes 124424 | tf_op jit(solution)/shard_map/ppermute | solution.py:13
  476.1 26.6 %collective-permute-start.52 = (f32[81,128]{1,0:T(8,128)}, f32[81,128]{1,0:T(8,128)}, u32[]{:S(2)}, u32[]{:S(2)}) collective-permute-start(f32[81,128]{1,0:T(8,128)} %bitcast.139), channel_id=1, source_target_pairs={{12,0},{13,1},{14,2},{15,3},{16,4},{17,5},{18,6},{19,7},{20,8},{21... | collective-permute-start | bytes 124424 | tf_op jit(solution)/shard_map/ppermute | solution.py:13
  477.4 27.2 %collective-permute-start.53 = (f32[81,128]{1,0:T(8,128)S(1)}, f32[81,128]{1,0:T(8,128)}, u32[]{:S(2)}, u32[]{:S(2)}) collective-permute-start(f32[81,128]{1,0:T(8,128)S(1)} %bitcast.313), channel_id=1, source_target_pairs={{13,0},{14,1},{15,2},{16,3},{17,4},{18,5},{19,6},{20,7},{21,8},{22... | collective-permute-start | bytes 124424 | tf_op jit(solution)/shard_map/ppermute | solution.py:13
  479.1 27.7 %collective-permute-start.28 = (f32[81,128]{1,0:T(8,128)S(1)}, f32[81,128]{1,0:T(8,128)S(1)}, u32[]{:S(2)}, u32[]{:S(2)}) collective-permute-start(f32[81,128]{1,0:T(8,128)S(1)} %bitcast.310), channel_id=1, source_target_pairs={{0,13},{1,14},{2,15},{3,16},{4,17},{5,18},{6,19},{7,20},{8,21},{9,... | collective-permute-start | bytes 124424 | tf_op jit(solution)/shard_map/ppermute | solution.py:13
  491.6 18.2 %collective-permute-start.29 = (f32[81,128]{1,0:T(8,128)S(1)}, f32[81,128]{1,0:T(8,128)}, u32[]{:S(2)}, u32[]{:S(2)}) collective-permute-start(f32[81,128]{1,0:T(8,128)S(1)} %bitcast.307), channel_id=1, source_target_pairs={{0,12},{1,13},{2,14},{3,15},{4,16},{5,17},{6,18},{7,19},{8,20},{9,... | collective-permute-start | bytes 124424 | tf_op jit(solution)/shard_map/ppermute | solution.py:13
  500.8 130.5 %collective-permute-start.30 = (f32[81,128]{1,0:T(8,128)S(1)}, f32[81,128]{1,0:T(8,128)}, u32[]{:S(2)}, u32[]{:S(2)}) collective-permute-start(f32[81,128]{1,0:T(8,128)S(1)} %bitcast.305), channel_id=1, source_target_pairs={{0,11},{1,12},{2,13},{3,14},{4,15},{5,16},{6,17},{7,18},{8,19},{9,... | collective-permute-start | bytes 124424 | tf_op jit(solution)/shard_map/ppermute | solution.py:13
  502.7 129.4 %collective-permute-start.31 = (f32[81,128]{1,0:T(8,128)S(1)}, f32[81,128]{1,0:T(8,128)}, u32[]{:S(2)}, u32[]{:S(2)}) collective-permute-start(f32[81,128]{1,0:T(8,128)S(1)} %bitcast.304), channel_id=1, source_target_pairs={{0,10},{1,11},{2,12},{3,13},{4,14},{5,15},{6,16},{7,17},{8,18},{9,... | collective-permute-start | bytes 124424 | tf_op jit(solution)/shard_map/ppermute | solution.py:13
  504.6 128.4 %collective-permute-start.32 = (f32[81,128]{1,0:T(8,128)S(1)}, f32[81,128]{1,0:T(8,128)}, u32[]{:S(2)}, u32[]{:S(2)}) collective-permute-start(f32[81,128]{1,0:T(8,128)S(1)} %bitcast.303), channel_id=1, source_target_pairs={{0,9},{1,10},{2,11},{3,12},{4,13},{5,14},{6,15},{7,16},{8,17},{9,1... | collective-permute-start | bytes 124424 | tf_op jit(solution)/shard_map/ppermute | solution.py:13
  506.8 126.9 %collective-permute-start.33 = (f32[81,128]{1,0:T(8,128)S(1)}, f32[81,128]{1,0:T(8,128)}, u32[]{:S(2)}, u32[]{:S(2)}) collective-permute-start(f32[81,128]{1,0:T(8,128)S(1)} %bitcast.302), channel_id=1, source_target_pairs={{0,8},{1,9},{2,10},{3,11},{4,12},{5,13},{6,14},{7,15},{8,16},{9,17... | collective-permute-start | bytes 124424 | tf_op jit(solution)/shard_map/ppermute | solution.py:13
  509.8 124.8 %collective-permute-start.34 = (f32[81,128]{1,0:T(8,128)S(1)}, f32[81,128]{1,0:T(8,128)S(1)}, u32[]{:S(2)}, u32[]{:S(2)}) collective-permute-start(f32[81,128]{1,0:T(8,128)S(1)} %bitcast.301), channel_id=1, source_target_pairs={{0,7},{1,8},{2,9},{3,10},{4,11},{5,12},{6,13},{7,14},{8,15},{9,16}... | collective-permute-start | bytes 124424 | tf_op jit(solution)/shard_map/ppermute | solution.py:13
  (82 other events, 1667.4 us)
where the time goes:
time: 675 us; the launch traced here: 663 us
  other arithmetic  228 us (34%)
  local copies, waits for them, and re-layouts  224 us (33%)
  starting transfers between devices  138 us (20%)
  matrix products  47.9 us (7%)
  waiting for transfers between devices  22.9 us (3%)
    ppermute x52, starting transfers between devices, shifted(): return lax.ppermute(block, axis, route)  134 us
    scatter-add x4, other arithmetic, shards(): outbound.at[:, source_cell]  93.5 us
    scatter-add x4, other arithmetic, shards(): near_local.at[:, target_cell].add(product[:, :, :slot_count] * live_mask)  91.1 us
    gather x4, local copies, waits for them, and re-layouts, shards(): extended[:, source_cell]  56.8 us
    gather x4, local copies, waits for them, and re-layouts, shards(): multipoles[:, target_cell] * parity_sign[:, None, None]  53.3 us
    dot_general x4, matrix products, shards(): jnp.einsum('ijk,jkq->ikq', m2l_ops[:, :, start_class:start_class + class_...  42.9 us
    unnamed x163, local copies, waits for them, and re-layouts  41.6 us
    ppermute x52, waiting for transfers between devices, shifted(): return lax.ppermute(block, axis, route)  22.9 us
  transfers between devices with their start and end apart: 54, of which 15 were waited for; matrix products, arithmetic and copies ran while one was open for 36% of the time, Pallas kernels for 0%

commit v1 on v0

v1 whole, which is shorter than its diff:
```python
import jax
import jax.numpy as jnp
from jax import lax
from jax.experimental import pallas as pl
from jax.experimental.pallas import tpu as pltpu
from jax.sharding import PartitionSpec as P

ORDER = 8
HALO = 16
LANES = 128
GROUP = 256
ACCS = 8
F32 = jnp.float32
BF16 = jnp.bfloat16
MAT_NT = (((1,), (1,)), ((), ()))


def split(value):
    high = value.astype(BF16)
    return high, (value - high.astype(F32)).astype(BF16)


def dot(a, b):
    return jnp.dot(a, b, preferred_element_type=F32)


def dot_nt(a, b):
    return lax.dot_general(a, b, MAT_NT, preferred_element_type=F32)


def pad_rows(value, rows):
    return jnp.concatenate(
        [value, jnp.zeros((rows - value.shape[0], value.shape[1]), value.dtype)], axis=0
    )


def parity_at(index):
    degree = jnp.zeros_like(index)
    for step in range(1, ORDER + 1):
        degree = degree + (index >= step * step).astype(jnp.int32)
    return (1 - 2 * (degree & 1)).astype(F32)


def peer_offset(slot, reach):
    return slot - reach if slot < reach else slot - reach + 1


def export_kernel(me, devices, reach, x_ref, idx_ref, out_ref):
    coeffs, cells = x_ref.shape
    rows = out_ref.shape[1]
    high, low = split(pad_rows(x_ref[...], rows))
    both = jnp.concatenate([high, low], axis=0)
    peers = idx_ref.shape[0]
    line = lax.broadcasted_iota(jnp.int32, (cells, LANES), 0)
    for slot in range(peers):
        other = me[0] + peer_offset(slot, reach)

        @pl.when(jnp.logical_and(other >= 0, other < devices))
        def _():
            hot = jnp.where(line == idx_ref[slot : slot + 1, :], 1.0, 0.0).astype(BF16)
            sent = dot(both, hot)
            out_ref[other] = sent[:rows] + sent[rows:]


def ops_kernel(m2l_ref, out_ref):
    coeffs = m2l_ref.shape[0]
    pitch = out_ref.shape[0] // LANES
    for i in range(coeffs):
        out_ref[pl.ds(i, LANES, pitch), :] = pad_rows(m2l_ref[i], LANES).T
    for i in range(coeffs, pitch):
        out_ref[pl.ds(i, LANES, pitch), :] = jnp.zeros((LANES, LANES), F32)


def weights_of(w_ref, start, pitch):
    high, low = split(pad_rows(w_ref[pl.ds(start, pitch), :], LANES))
    return jnp.concatenate(
        [jnp.concatenate([high, high], axis=1), jnp.concatenate([low, low], axis=1)], axis=0
    )


def products(columns, w_ref, first, pitch, slots):
    parts = []
    for k in range(GROUP // slots):
        start = pl.multiple_of((first + k) * pitch, 8)
        y = dot_nt(columns[k * slots : (k + 1) * slots], weights_of(w_ref, start, pitch))
        parts.append(y[:, :LANES] + y[:, LANES:])
    return jnp.concatenate(parts, axis=0)


def source_kernel(devices, reach, slots, me, src, x_ref, tgt_ref, w_ref, ret_ref, own_ref, table, bufs, accs):
    step = pl.program_id(0)
    steps = pl.num_programs(0)
    coeffs, cells = x_ref.shape
    groups = tgt_ref.shape[2]
    classes = GROUP // slots
    pitch = w_ref.shape[0] // (groups * classes)

    @pl.when(step == 0)
    def _():
        sign = parity_at(lax.broadcasted_iota(jnp.int32, (coeffs, cells), 0))
        high, low = split(pad_rows(x_ref[...] * sign, LANES).T)
        table[:, :LANES] = high
        table[:, LANES:] = low
        for acc in accs:
            acc[...] = jnp.zeros_like(acc)

    line = lax.broadcasted_iota(jnp.int32, (GROUP, cells), 1)

    def compute(g):
        hot = jnp.where(tgt_ref[0, :, g : g + 1] == line, 1.0, 0.0).astype(BF16)
        columns = dot(hot, table[...]).astype(BF16)
        bufs[g % 2][...] = products(columns, w_ref, g * classes, pitch, slots)

    def scatter(buf, base):
        for q in range(GROUP):
            acc = accs[q % len(accs)]
            row = src[base + q]
            acc[pl.ds(row, 1), :] += buf[q : q + 1, :]

    base = step * (groups * GROUP)
    compute(0)
    for g in range(1, groups):
        compute(g)
        scatter(bufs[(g - 1) % 2], base + (g - 1) * GROUP)
    scatter(bufs[(groups - 1) % 2], base + (groups - 1) * GROUP)

    @pl.when(step == steps - 1)
    def _():
        sign = parity_at(lax.broadcasted_iota(jnp.int32, (LANES, LANES), 1))

        def total(start):
            value = accs[0][start : start + LANES, :]
            for acc in accs[1:]:
                value = value + acc[start : start + LANES, :]
            return value * sign

        for start in range(0, cells, LANES):
            own_ref[start : start + LANES, :] = total(start)
        rows = ret_ref.shape[1]
        for slot in range((accs[0].shape[0] - cells) // LANES):
            other = me[0] + peer_offset(slot, reach)

            @pl.when(jnp.logical_and(other >= 0, other < devices))
            def _():
                ret_ref[other] = total(cells + slot * LANES).T[:rows]


def target_kernel(
    devices, reach, slots, me, src, x_ref, got_ref, tgt_ref, w_ref, own_ref, par_ref, pos_ref, oct_ref, l2l_ref,
    out_ref, table, near, bufs,
):
    step = pl.program_id(0)
    steps = pl.num_programs(0)
    coeffs, cells = x_ref.shape
    groups = tgt_ref.shape[1]
    classes = GROUP // slots
    pitch = w_ref.shape[0] // (groups * classes)

    @pl.when(step == 0)
    def _():
        table[:cells, :] = pad_rows(x_ref[...], LANES).T
        for slot in range((table.shape[0] - cells) // LANES):
            other = jnp.clip(me[0] + peer_offset(slot, reach), 0, devices - 1)
            start = cells + slot * LANES
            table[start : start + LANES, :] = pad_rows(got_ref[other], LANES).T
        near[...] = jnp.zeros_like(near)

    line = lax.broadcasted_iota(jnp.int32, (cells, GROUP), 0)

    def gather(buf, base):
        for q in range(GROUP):
            buf[q : q + 1, :] = table[pl.ds(src[base + q], 1), :]

    def compute(g):
        high, low = split(bufs[g % 2][...])
        y = products(jnp.concatenate([high, low], axis=1), w_ref, g * classes, pitch, slots)
        hot = jnp.where(tgt_ref[0, g : g + 1, :] == line, 1.0, 0.0).astype(BF16)
        near[...] += dot(hot, jnp.concatenate(split(y), axis=1))

    base = step * (groups * GROUP)
    gather(bufs[0], base)
    for g in range(groups):
        if g + 1 < groups:
            gather(bufs[(g + 1) % 2], base + (g + 1) * GROUP)
        compute(g)

    @pl.when(step == steps - 1)
    def _():
        wide = par_ref.shape[1]
        parents = jnp.concatenate(split(pad_rows(par_ref[...], LANES)), axis=0)
        hot = jnp.where(
            pos_ref[...] == lax.broadcasted_iota(jnp.int32, (wide, cells), 0), 1.0, 0.0
        ).astype(BF16)
        picked = dot(parents, hot).astype(BF16)
        total = (near[:, :LANES] + near[:, LANES:] + own_ref[...]).T[:coeffs]
        for k in range(l2l_ref.shape[0]):
            high, low = split(l2l_ref[k])
            filler = jnp.zeros((coeffs, LANES - coeffs), BF16)
            rows = jnp.concatenate([high, filler, high, filler], axis=1)
            term = dot(rows, picked)
            rows = jnp.concatenate([low, filler], axis=1)
            term = term + dot(rows, picked[:LANES])
            total = total + jnp.where(oct_ref[...] == k, term, 0.0)
        out_ref[...] = total


def back_kernel(devices, reach, me, base_ref, got_ref, idx_ref, out_ref, total):
    coeffs, cells = base_ref.shape
    rows = got_ref.shape[1]
    total[...] = jnp.zeros_like(total)
    line = lax.broadcasted_iota(jnp.int32, (cells, LANES), 0)
    for slot in range(idx_ref.shape[0]):
        other = me[0] + peer_offset(slot, reach)

        @pl.when(jnp.logical_and(other >= 0, other < devices))
        def _():
            hot = jnp.where(line == idx_ref[slot : slot + 1, :], 1.0, 0.0).astype(BF16)
            both = jnp.concatenate(split(got_ref[other]), axis=0)
            total[...] += dot_nt(both, hot)

    out_ref[...] = base_ref[...] + total[:coeffs] + total[rows : rows + coeffs]


def padded_2(shard, axis, width):
    size, length = lax.axis_size(axis), shard.shape[1]
    up = [(i, i + 1) for i in range(size - 1)]
    down = [(j, i) for i, j in up]
    before = lax.ppermute(shard[:, length - width :], axis, up)
    after = lax.ppermute(shard[:, :width], axis, down)
    return jnp.concatenate([before, shard, after], axis=1)


def vmem():
    return pl.BlockSpec(memory_space=pltpu.VMEM)


def smem():
    return pl.BlockSpec(memory_space=pltpu.SMEM)


LIMIT = 56 * 1024 * 1024


def shards(
    multipoles, parent_locals, m2l_ops, l2l_ops, export_cells, pair_first, pair_second, pair_count, parent_of, octant
):
    axes = ("gx", "gy")
    coeffs, cells = multipoles.shape
    exported = export_cells[0]
    peers, send = exported.shape
    reach = peers // 2
    classes = m2l_ops.shape[2]
    slots = pair_first.shape[2]
    devices = lax.axis_size("gx") * lax.axis_size("gy")
    position = lax.axis_index("gx") * lax.axis_size("gy") + lax.axis_index("gy")
    me = position.reshape(1).astype(jnp.int32)
    rows = -(-coeffs // 8) * 8
    steps = 16
    groups = classes * slots // (GROUP * steps)

    outgoing = pl.pallas_call(
        lambda me, *refs: export_kernel(me, devices, reach, *refs),
        out_shape=jax.ShapeDtypeStruct((devices, rows, send), F32),
        in_specs=[smem(), vmem(), vmem()],
        out_specs=vmem(),
        compiler_params=pltpu.CompilerParams(vmem_limit_bytes=LIMIT),
        cost_estimate=pl.CostEstimate(flops=10**9, bytes_accessed=2 * 10**6, transcendentals=0),
        name="exports",
    )(me, multipoles, exported)
    arrived = lax.all_to_all(outgoing, axes, 0, 0, tiled=True)
    padded = padded_2(parent_locals, axes, HALO)

    weights = pl.pallas_call(
        ops_kernel,
        out_shape=jax.ShapeDtypeStruct((classes * rows, LANES), F32),
        grid=(classes // LANES,),
        in_specs=[pl.BlockSpec((coeffs, coeffs, LANES), lambda s: (0, 0, s))],
        out_specs=pl.BlockSpec((LANES * rows, LANES), lambda s: (s, 0)),
        compiler_params=pltpu.CompilerParams(vmem_limit_bytes=LIMIT),
        cost_estimate=pl.CostEstimate(flops=10**9, bytes_accessed=20 * 10**6, transcendentals=0),
        name="operators",
    )(m2l_ops)

    live = lax.broadcasted_iota(jnp.int32, (classes, slots), 1) < pair_count[0][:, None]
    target = jnp.where(live, pair_first[0], -1)
    target_rows = target.reshape(steps, groups, GROUP)
    target_columns = jnp.transpose(target_rows, (0, 2, 1))
    source = pair_second[0].reshape(-1)

    w_spec = pl.BlockSpec((groups * GROUP // slots * rows, LANES), lambda s, *_: (s, 0))
    whole = pl.BlockSpec(memory_space=pltpu.VMEM)
    returned, own = pl.pallas_call(
        lambda me, src, x, t, w, r, o, table, b0, b1, *accs: source_kernel(
            devices, reach, slots, me, src, x, t, w, r, o, table, (b0, b1), accs
        ),
        out_shape=(
            jax.ShapeDtypeStruct((devices, rows, send), F32),
            jax.ShapeDtypeStruct((cells, LANES), F32),
        ),
        grid_spec=pltpu.PrefetchScalarGridSpec(
            num_scalar_prefetch=2,
            grid=(steps,),
            in_specs=[whole, pl.BlockSpec((1, GROUP, groups), lambda s, *_: (s, 0, 0)), w_spec],
            out_specs=(whole, whole),
            scratch_shapes=[
                pltpu.VMEM((cells, 2 * LANES), BF16),
                pltpu.VMEM((GROUP, LANES), F32),
                pltpu.VMEM((GROUP, LANES), F32),
            ]
            + [pltpu.VMEM((cells + peers * send, LANES), F32)] * ACCS,
        ),
        compiler_params=pltpu.CompilerParams(vmem_limit_bytes=LIMIT),
        cost_estimate=pl.CostEstimate(flops=20 * 10**9, bytes_accessed=50 * 10**6, transcendentals=0),
        name="to_source",
    )(me, source, multipoles, target_columns, weights)
    back = lax.all_to_all(returned, axes, 0, 0, tiled=True)

    place = (parent_of - position * parent_locals.shape[1] + HALO).reshape(1, cells)
    base = pl.pallas_call(
        lambda *refs: target_kernel(devices, reach, slots, *refs[:14], refs[14:]),
        out_shape=jax.ShapeDtypeStruct((coeffs, cells), F32),
        grid_spec=pltpu.PrefetchScalarGridSpec(
            num_scalar_prefetch=2,
            grid=(steps,),
            in_specs=[whole, whole, pl.BlockSpec((1, groups, GROUP), lambda s, *_: (s, 0, 0)), w_spec]
            + [whole] * 5,
            out_specs=whole,
            scratch_shapes=[
                pltpu.VMEM((cells + peers * send, LANES), F32),
                pltpu.VMEM((cells, 2 * LANES), F32),
                pltpu.VMEM((GROUP, LANES), F32),
                pltpu.VMEM((GROUP, LANES), F32),
            ],
        ),
        compiler_params=pltpu.CompilerParams(vmem_limit_bytes=LIMIT),
        cost_estimate=pl.CostEstimate(flops=20 * 10**9, bytes_accessed=50 * 10**6, transcendentals=0),
        name="to_target",
    )(me, source, multipoles, arrived, target_rows, weights, own, padded, place, octant.reshape(1, cells), l2l_ops)

    return pl.pallas_call(
        lambda me, *refs: back_kernel(devices, reach, me, *refs),
        out_shape=jax.ShapeDtypeStruct((coeffs, cells), F32),
        in_specs=[smem(), vmem(), vmem(), vmem()],
        out_specs=vmem(),
        scratch_shapes=[pltpu.VMEM((2 * rows, cells), F32)],
        compiler_params=pltpu.CompilerParams(vmem_limit_bytes=LIMIT),
        cost_estimate=pl.CostEstimate(flops=10**9, bytes_accessed=2 * 10**6, transcendentals=0),
        name="returned",
    )(me, base, back, exported)


def solution(mesh):
    placed = (
        P(None, ("gx", "gy")),
        P(None, ("gx", "gy")),
        P(),
        P(),
        P(("gx", "gy"), None, None),
        P(("gx", "gy"), None, None),
        P(("gx", "gy"), None, None),
        P(("gx", "gy"), None),
        P(("gx", "gy")),
        P(("gx", "gy")),
    )
    return jax.shard_map(
        shards, mesh=mesh, in_specs=placed, out_specs=P(None, ("gx", "gy")), check_vma=False
    )
```

time: 675 us -> 145 us (0.21)
  the two profiles are of different devices: /device:TPU:0 before, /device:TPU:17 now
where the time goes in v1:
time: 145 us
  Pallas kernels  90.1 us (62%)
  waiting for transfers between devices  26.7 us (18%)
  starting transfers between devices  17.2 us (12%)
  local copies, waits for them, and re-layouts  8.63 us (6%)
  other arithmetic  1.98 us (1%)
    pallas_call x1, Pallas kernels, shards(): pl.pallas_call(lambda *refs: target_kernel(devices, reach, slots, *refs[:...  36 us
    pallas_call x1, Pallas kernels, shards(): pl.pallas_call(lambda me, src, x, t, w, r, o, table, b0, b1, *accs: sourc...  31.9 us
    ppermute x1, waiting for transfers between devices, padded_2(): before = lax.ppermute(shard[:, length - width:], axis, up)  26.7 us
    pallas_call x1, Pallas kernels, shards(): pl.pallas_call(ops_kernel, out_shape=jax.ShapeDtypeStruct((classes * rows...  7.85 us
    pallas_call x1, Pallas kernels, shards(): pl.pallas_call(lambda me, *refs: back_kernel(devices, reach, me, *refs),...  7.35 us
    pallas_call x1, Pallas kernels, shards(): pl.pallas_call(lambda me, *refs: export_kernel(me, devices, reach, *refs)...  6.96 us
    all_to_all x1, starting transfers between devices, shards(): arrived = lax.all_to_all(outgoing, axes, 0, 0, tiled=True)  5.51 us
    all_to_all x1, starting transfers between devices, shards(): back = lax.all_to_all(returned, axes, 0, 0, tiled=True)  5.5 us
  transfers between devices with their start and end apart: 4, of which 1 were waited for; matrix products, arithmetic and copies ran while one was open for 5% of the time, Pallas kernels for 52%

profile of v1, /device:TPU:17, one launch (start us, length us, event | category | flops | bytes accessed | tf_op | source)
XLA Modules:
  0.0 144.8 jit_solution(4925804826174649464)
XLA Ops:
  0.0 1.3 copy.26
  1.3 7.0 %exports.1 = f32[32,88,128]{2,1,0:T(8,128)} custom-call(s32[1]{0:T(128)} %bitcast.me.refs_0_, f32[81,512]{1,0:T(8,128)} %refs_2_.1, s32[26,128]{1,0:T(8,128)} %bitcast.8), custom_call_target="tpu_custom_call" | custom-call | flops 1000000000 | bytes 2000000 | tf_op jit(solution)/shard_map/exports/pallas_call | solution.py:261
  8.3 5.5 %all-to-all-start = ((f32[32,88,128]{2,1,0:T(8,128)}), f32[32,88,128]{2,1,0:T(8,128)S(1)}, u32[]{:S(2)}, u32[]{:S(2)}) async-start(f32[32,88,128]{2,1,0:T(8,128)} %exports.1), calls=%async_computation | async-start | bytes 2883584 | tf_op jit(solution)/shard_map/all_to_all | solution.py:270
  13.8 0.5 broadcast.8
  14.3 0.7 reduce.3
  15.0 0.1 lt.13
  15.1 0.1 lt.14
  15.2 0.1 lt.15
  15.5 0.1 squeeze.7
  15.7 2.1 %copy.19.t = s32[16,256,4]{2,1,0:T(8,128)} copy(s32[16,256,4]{1,2,0:T(4,128)S(1)} %bitcast.7) | data formatting | bytes 131072 | tf_op jit(solution)/shard_map/transpose | solution.py:287
  17.9 0.7 reshape_squeeze.3.src.refs_1_
  18.6 7.9 %operators.1.w.refs_5_ = f32[22528,128]{1,0:T(8,128)} custom-call(f32[81,81,256]{2,1,0:T(8,128)} %m2l_ref.1), custom_call_target="tpu_custom_call" | custom-call | flops 1000000000 | bytes 20000000 | tf_op jit(solution)/shard_map/operators/pallas_call | solution.py:273
  26.5 31.9 %to_source.1 = (f32[32,88,128]{2,1,0:T(8,128)}, f32[512,128]{1,0:T(8,128)}) custom-call(s32[1]{0:T(128)} %bitcast.me.refs_0_, s32[16384]{0:T(1024)} %reshape_squeeze.3.src.refs_1_, f32[81,512]{1,0:T(8,128)} %refs_2_.1, s32[16,256,4]{2,1,0:T(8,128)} %copy.19.t, f32[22528,128]{1,0:T(8,128)} %operators.1.w.refs_5_), custom_call_target="tpu_custom_call" | custom-call | flops 20000000000 | bytes 50000000 | tf_op jit(solution)/shard_map/to_source/pallas_call | solution.py:292
  58.5 1.1 copy-done
  59.6 5.5 %all-to-all-start.1 = ((f32[32,88,128]{2,1,0:T(8,128)}), f32[32,88,128]{2,1,0:T(8,128)S(1)}, u32[]{:S(2)}, u32[]{:S(2)}) async-start(f32[32,88,128]{2,1,0:T(8,128)} %get-tuple-element.8), calls=%async_computation.1 | async-start | bytes 2883584 | tf_op jit(solution)/shard_map/all_to_all | solution.py:316
  65.3 3.1 %collective-permute-start = (f32[81,16]{1,0:T(8,128)S(1)}, f32[81,16]{1,0:T(8,128)S(1)}, u32[]{:S(2)}, u32[]{:S(2)}) collective-permute-start(f32[81,16]{1,0:T(8,128)S(1)} %get-tuple-element.9), channel_id=1, source_target_pairs={{0,1},{1,2},{2,3},{3,4},{4,5},{5,6},{6,7},{7,8},{8,9},{9,10},{10,1... | collective-permute-start | bytes 15560 | tf_op jit(solution)/shard_map/ppermute | solution.py:228
  68.4 3.1 %collective-permute-start.1 = (f32[81,16]{1,0:T(8,128)S(1)}, f32[81,16]{1,0:T(8,128)S(1)}, u32[]{:S(2)}, u32[]{:S(2)}) collective-permute-start(f32[81,16]{1,0:T(8,128)S(1)} %get-tuple-element.10), channel_id=1, source_target_pairs={{1,0},{2,1},{3,2},{4,3},{5,4},{6,5},{7,6},{8,7},{9,8},{10,9},{11,1... | collective-permute-start | bytes 15560 | tf_op jit(solution)/shard_map/ppermute | solution.py:229
  71.5 0.6 subtract_add_fusion
  72.1 0.8 copy.23.refs_10_
  72.9 26.7 %collective-permute-done = f32[81,16]{1,0:T(8,128)S(1)} collective-permute-done((f32[81,16]{1,0:T(8,128)S(1)}, f32[81,16]{1,0:T(8,128)S(1)}, u32[]{:S(2)}, u32[]{:S(2)}) %collective-permute-start) | collective-permute-done | bytes 5216 | tf_op jit(solution)/shard_map/ppermute | solution.py:228
  99.6 0.7 pad_maximum_fusion.refs_7_
  100.3 36.0 %to_target.1.refs_0_ = f32[81,512]{1,0:T(8,128)} custom-call(s32[1]{0:T(128)} %bitcast.me.refs_0_, s32[16384]{0:T(1024)} %reshape_squeeze.3.src.refs_1_, f32[81,512]{1,0:T(8,128)} %refs_2_.1, f32[32,88,128]{2,1,0:T(8,128)} %copy-done, s32[16,4,256]{2,1,0:T(4,128)} %copy-done.3, f32[22528,128]{1,0:T(8,128)} %operators.1.w.refs_5_, ...), custom_call_target="tpu_custom_call" | custom-call | flops 20000000000 | bytes 50000000 | tf_op jit(solution)/shard_map/to_target/pallas_call | solution.py:319
  136.3 1.1 copy-done.1
  137.4 7.4 %returned.1 = f32[81,512]{1,0:T(8,128)} custom-call(s32[1]{0:T(128)} %bitcast.me.refs_0_, f32[81,512]{1,0:T(8,128)} %to_target.1.refs_0_, f32[32,88,128]{2,1,0:T(8,128)} %copy-done.1, s32[26,128]{1,0:T(8,128)} %bitcast.9), custom_call_target="tpu_custom_call" | custom-call | flops 1000000000 | bytes 2000000 | tf_op jit(solution)/shard_map/returned/pallas_call | solution.py:340
  (26 shorter events, 0.5 us)
Async XLA Ops:
  8.3 6.0 %copy-start.8 = (s32[1,256]{1,0:T(1,128)S(1)}, s32[1,256]{1,0:T(1,128)}, u32[]{:S(2)}) copy-start(s32[1,256]{1,0:T(1,128)} %param.17) | copy-start | bytes 3076
  8.3 7.1 %copy-start.4 = (s32[1,256,64]{1,2,0:T(8,128)S(1)}, s32[1,256,64]{1,2,0:T(8,128)}, u32[]{:S(2)}) copy-start(s32[1,256,64]{1,2,0:T(8,128)} %param.15) | copy-start | bytes 196612
  8.3 50.2 %all-to-all-start = ((f32[32,88,128]{2,1,0:T(8,128)}), f32[32,88,128]{2,1,0:T(8,128)S(1)}, u32[]{:S(2)}, u32[]{:S(2)}) async-start(f32[32,88,128]{2,1,0:T(8,128)} %exports.1), calls=%async_computation | async-start | bytes 2883584 | tf_op jit(solution)/shard_map/all_to_all | solution.py:270
  15.2 2.6 %copy-start.5 = (s32[1,256,64]{1,2,0:T(8,128)S(1)}, s32[1,256,64]{1,2,0:T(8,128)}, u32[]{:S(2)}) copy-start(s32[1,256,64]{1,2,0:T(8,128)} %param.16) | copy-start | bytes 196612
  15.7 10.8 %copy-start.3 = (s32[16,4,256]{2,1,0:T(4,128)}, s32[16,4,256]{2,1,0:T(4,128)S(1)}, u32[]{:S(2)}) copy-start(s32[16,4,256]{2,1,0:T(4,128)S(1)} %compare_select_fusion.refs_4_) | copy-start | bytes 196612
  58.4 1.1 copy-start
  58.4 6.7 %copy-start.6 = (f32[81,64]{0,1:T(8,128)S(1)}, f32[81,64]{0,1:T(8,128)}, u32[]{:S(2)}) copy-start(f32[81,64]{0,1:T(8,128)} %param.11) | copy-start | bytes 62212
  58.5 13.0 %copy-start.7 = (s32[512]{0:T(512)S(1)}, s32[512]{0:T(512)}, u32[]{:S(2)}) copy-start(s32[512]{0:T(512)} %param.18) | copy-start | bytes 6148
  58.5 13.6 %copy-start.2 = (f32[8,81,81]{2,0,1:T(8,128)S(1)}, f32[8,81,81]{2,0,1:T(8,128)}, u32[]{:S(2)}) copy-start(f32[8,81,81]{2,0,1:T(8,128)} %param.13) | copy-start | bytes 629860
  59.6 76.7 %all-to-all-start.1 = ((f32[32,88,128]{2,1,0:T(8,128)}), f32[32,88,128]{2,1,0:T(8,128)S(1)}, u32[]{:S(2)}, u32[]{:S(2)}) async-start(f32[32,88,128]{2,1,0:T(8,128)} %get-tuple-element.8), calls=%async_computation.1 | async-start | bytes 2883584 | tf_op jit(solution)/shard_map/all_to_all | solution.py:316
  65.3 34.3 %collective-permute-start = (f32[81,16]{1,0:T(8,128)S(1)}, f32[81,16]{1,0:T(8,128)S(1)}, u32[]{:S(2)}, u32[]{:S(2)}) collective-permute-start(f32[81,16]{1,0:T(8,128)S(1)} %get-tuple-element.9), channel_id=1, source_target_pairs={{0,1},{1,2},{2,3},{3,4},{4,5},{5,6},{6,7},{7,8},{8,9},{9,10},{10,1... | collective-permute-start | bytes 15560 | tf_op jit(solution)/shard_map/ppermute | solution.py:228
  68.4 31.2 %collective-permute-start.1 = (f32[81,16]{1,0:T(8,128)S(1)}, f32[81,16]{1,0:T(8,128)S(1)}, u32[]{:S(2)}, u32[]{:S(2)}) collective-permute-start(f32[81,16]{1,0:T(8,128)S(1)} %get-tuple-element.10), channel_id=1, source_target_pairs={{1,0},{2,1},{3,2},{4,3},{5,4},{6,5},{7,6},{8,7},{9,8},{10,9},{11,1... | collective-permute-start | bytes 15560 | tf_op jit(solution)/shard_map/ppermute | solution.py:229
  136.3 1.1 copy-start.1

commit v2 on v1

--- a/solution.py
+++ b/solution.py
@@ -45,12 +45,61 @@
     return slot - reach if slot < reach else slot - reach + 1
 
 
-def export_kernel(me, devices, reach, x_ref, idx_ref, out_ref):
+def stacked(value, coeffs):
+    head = coeffs - 1
+    high = value.astype(BF16).astype(F32)
+    low = value - high
+    row = lax.broadcasted_iota(jnp.int32, (2 * LANES - 3 * head, value.shape[1]), 0)
+    last = jnp.where(row == 1, low[head:], jnp.where(row < 3, high[head:], 0.0))
+    return jnp.concatenate([high[:head], low[:head], high[:head], last], axis=0)
+
+
+def tagged(value, coeffs):
+    head = coeffs - 1
+    last = value[head : head + 1]
+    row = lax.broadcasted_iota(jnp.int32, (LANES - head, value.shape[1]), 0)
+    low = last - last.astype(BF16).astype(F32)
+    tail = jnp.where(row == 1, low, jnp.where(row < 3, last, 0.0))
+    return jnp.concatenate([value[:head], tail], axis=0)
+
+
+def paired(rows, coeffs):
+    head = coeffs - 1
+    high = rows.astype(BF16).astype(F32)
+    low = pltpu.roll(rows - high, head, 1)
+    again = pltpu.roll(high, 2 * head - LANES, 1)
+    lane = lax.broadcasted_iota(jnp.int32, rows.shape, 1)
+    left = jnp.where(lane < head, high, low)
+    right = jnp.where(lane < 2 * head - LANES, low, again)
+    return jnp.concatenate([left, right], axis=1).astype(BF16)
+
+
+def halo_out(rows, coeffs):
+    lane = lax.broadcasted_iota(jnp.int32, (1, LANES), 1)
+    room = LANES - coeffs
+    last = rows[HALO - 1 :]
+    first = jnp.where(lane < coeffs, rows[:1], pltpu.roll(last, coeffs, 1))
+    second = jnp.where(lane < coeffs, rows[1:2], pltpu.roll(last, coeffs - room, 1))
+    return jnp.concatenate([first, second, rows[2 : HALO - 1]], axis=0)
+
+
+def halo_in(sent, coeffs):
+    lane = lax.broadcasted_iota(jnp.int32, (1, LANES), 1)
+    room = LANES - coeffs
+    last = jnp.where(
+        lane < room, pltpu.roll(sent[:1], room, 1), pltpu.roll(sent[1:2], LANES + room - coeffs, 1)
+    )
+    rows = jnp.concatenate([sent, last], axis=0)
+    return jnp.where(lax.broadcasted_iota(jnp.int32, rows.shape, 1) < coeffs, rows, 0.0)
+
+
+def export_kernel(me, devices, reach, x_ref, idx_ref, par_ref, out_ref):
     coeffs, cells = x_ref.shape
-    rows = out_ref.shape[1]
+    rows = -(-coeffs // 8) * 8
     high, low = split(pad_rows(x_ref[...], rows))
     both = jnp.concatenate([high, low], axis=0)
     peers = idx_ref.shape[0]
+    parents = pad_rows(par_ref[...], LANES).T
     line = lax.broadcasted_iota(jnp.int32, (cells, LANES), 0)
     for slot in range(peers):
         other = me[0] + peer_offset(slot, reach)
@@ -59,32 +108,45 @@
         def _():
             hot = jnp.where(line == idx_ref[slot : slot + 1, :], 1.0, 0.0).astype(BF16)
             sent = dot(both, hot)
-            out_ref[other] = sent[:rows] + sent[rows:]
-
-
-def ops_kernel(m2l_ref, out_ref):
+            out_ref[other, :rows] = sent[:rows] + sent[rows:]
+            if slot == reach - 1:
+                out_ref[other, coeffs : coeffs + HALO - 1] = halo_out(parents[:HALO], coeffs)
+            if slot == reach:
+                out_ref[other, coeffs : coeffs + HALO - 1] = halo_out(parents[-HALO:], coeffs)
+
+
+def ops_kernel(m2l_ref, out_ref, turned):
     coeffs = m2l_ref.shape[0]
     pitch = out_ref.shape[0] // LANES
     for i in range(coeffs):
-        out_ref[pl.ds(i, LANES, pitch), :] = pad_rows(m2l_ref[i], LANES).T
-    for i in range(coeffs, pitch):
-        out_ref[pl.ds(i, LANES, pitch), :] = jnp.zeros((LANES, LANES), F32)
-
-
-def weights_of(w_ref, start, pitch):
-    high, low = split(pad_rows(w_ref[pl.ds(start, pitch), :], LANES))
+        turned[pl.ds(i, pitch, pitch), :] = pad_rows(m2l_ref[i], pitch)
+    for j in range(coeffs):
+        block = pad_rows(turned[j * pitch : j * pitch + coeffs, :], LANES).T
+        out_ref[pl.ds(j, LANES, pitch), :] = block
+    out_ref[pl.ds(coeffs, LANES, pitch), :] = block
+    out_ref[pl.ds(coeffs + 1, LANES, pitch), :] = block - block.astype(BF16).astype(F32)
+    for j in range(coeffs + 2, pitch):
+        out_ref[pl.ds(j, LANES, pitch), :] = jnp.zeros((LANES, LANES), F32)
+
+
+def weights_of(w_ref, start, pitch, coeffs):
+    head = coeffs - 1
+    high, low = split(w_ref[pl.ds(start, head), :])
+    last = pad_rows(w_ref[pl.ds(start + head, pitch - head), :], 2 * LANES - 3 * head).astype(BF16)
+    return jnp.concatenate([high, high, low, last], axis=0)
+
+
+def products(columns, w_ref, first, pitch, slots, coeffs):
     return jnp.concatenate(
-        [jnp.concatenate([high, high], axis=1), jnp.concatenate([low, low], axis=1)], axis=0
+        [
+            dot(
+                columns[k * slots : (k + 1) * slots],
+                weights_of(w_ref, (first + k) * pitch, pitch, coeffs),
+            )
+            for k in range(GROUP // slots)
+        ],
+        axis=0,
     )
-
-
-def products(columns, w_ref, first, pitch, slots):
-    parts = []
-    for k in range(GROUP // slots):
-        start = pl.multiple_of((first + k) * pitch, 8)
-        y = dot_nt(columns[k * slots : (k + 1) * slots], weights_of(w_ref, start, pitch))
-        parts.append(y[:, :LANES] + y[:, LANES:])
-    return jnp.concatenate(parts, axis=0)
 
 
 def source_kernel(devices, reach, slots, me, src, x_ref, tgt_ref, w_ref, ret_ref, own_ref, table, bufs, accs):
@@ -98,9 +160,7 @@
     @pl.when(step == 0)
     def _():
         sign = parity_at(lax.broadcasted_iota(jnp.int32, (coeffs, cells), 0))
-        high, low = split(pad_rows(x_ref[...] * sign, LANES).T)
-        table[:, :LANES] = high
-        table[:, LANES:] = low
+        table[...] = stacked(x_ref[...] * sign, coeffs).T.astype(BF16)
         for acc in accs:
             acc[...] = jnp.zeros_like(acc)
 
@@ -109,7 +169,7 @@
     def compute(g):
         hot = jnp.where(tgt_ref[0, :, g : g + 1] == line, 1.0, 0.0).astype(BF16)
         columns = dot(hot, table[...]).astype(BF16)
-        bufs[g % 2][...] = products(columns, w_ref, g * classes, pitch, slots)
+        bufs[g % 2][...] = products(columns, w_ref, g * classes, pitch, slots, coeffs)
 
     def scatter(buf, base):
         for q in range(GROUP):
@@ -158,11 +218,11 @@
 
     @pl.when(step == 0)
     def _():
-        table[:cells, :] = pad_rows(x_ref[...], LANES).T
+        table[:cells, :] = tagged(x_ref[...], coeffs).T
         for slot in range((table.shape[0] - cells) // LANES):
             other = jnp.clip(me[0] + peer_offset(slot, reach), 0, devices - 1)
             start = cells + slot * LANES
-            table[start : start + LANES, :] = pad_rows(got_ref[other], LANES).T
+            table[start : start + LANES, :] = tagged(got_ref[other, :coeffs], coeffs).T
         near[...] = jnp.zeros_like(near)
 
     line = lax.broadcasted_iota(jnp.int32, (cells, GROUP), 0)
@@ -172,8 +232,7 @@
             buf[q : q + 1, :] = table[pl.ds(src[base + q], 1), :]
 
     def compute(g):
-        high, low = split(bufs[g % 2][...])
-        y = products(jnp.concatenate([high, low], axis=1), w_ref, g * classes, pitch, slots)
+        y = products(paired(bufs[g % 2][...], coeffs), w_ref, g * classes, pitch, slots, coeffs)
         hot = jnp.where(tgt_ref[0, g : g + 1, :] == line, 1.0, 0.0).astype(BF16)
         near[...] += dot(hot, jnp.concatenate(split(y), axis=1))
 
@@ -186,8 +245,14 @@
 
     @pl.when(step == steps - 1)
     def _():
-        wide = par_ref.shape[1]
-        parents = jnp.concatenate(split(pad_rows(par_ref[...], LANES)), axis=0)
+        parts = [None, pad_rows(par_ref[...], LANES).T, None]
+        for part, shift in ((0, -1), (2, 1)):
+            other = jnp.clip(me[0] + shift, 0, devices - 1)
+            sent = halo_in(got_ref[other, coeffs : coeffs + HALO - 1], coeffs)
+            parts[part] = jnp.where(other == me[0], 0.0, sent)
+        parents = jnp.concatenate(parts, axis=0)
+        wide = parents.shape[0]
+        parents = jnp.concatenate(split(parents.T), axis=0)
         hot = jnp.where(
             pos_ref[...] == lax.broadcasted_iota(jnp.int32, (wide, cells), 0), 1.0, 0.0
         ).astype(BF16)
@@ -219,15 +284,6 @@
             total[...] += dot_nt(both, hot)
 
     out_ref[...] = base_ref[...] + total[:coeffs] + total[rows : rows + coeffs]
-
-
-def padded_2(shard, axis, width):
-    size, length = lax.axis_size(axis), shard.shape[1]
-    up = [(i, i + 1) for i in range(size - 1)]
-    down = [(j, i) for i, j in up]
-    before = lax.ppermute(shard[:, length - width :], axis, up)
-    after = lax.ppermute(shard[:, :width], axis, down)
-    return jnp.concatenate([before, shard, after], axis=1)
 
 
 def vmem():
@@ -260,15 +316,14 @@
 
     outgoing = pl.pallas_call(
         lambda me, *refs: export_kernel(me, devices, reach, *refs),
-        out_shape=jax.ShapeDtypeStruct((devices, rows, send), F32),
-        in_specs=[smem(), vmem(), vmem()],
+        out_shape=jax.ShapeDtypeStruct((devices, coeffs + HALO - 1, send), F32),
+        in_specs=[smem(), vmem(), vmem(), vmem()],
         out_specs=vmem(),
         compiler_params=pltpu.CompilerParams(vmem_limit_bytes=LIMIT),
         cost_estimate=pl.CostEstimate(flops=10**9, bytes_accessed=2 * 10**6, transcendentals=0),
         name="exports",
-    )(me, multipoles, exported)
+    )(me, multipoles, exported, parent_locals)
     arrived = lax.all_to_all(outgoing, axes, 0, 0, tiled=True)
-    padded = padded_2(parent_locals, axes, HALO)
 
     weights = pl.pallas_call(
         ops_kernel,
@@ -276,6 +331,7 @@
         grid=(classes // LANES,),
         in_specs=[pl.BlockSpec((coeffs, coeffs, LANES), lambda s: (0, 0, s))],
         out_specs=pl.BlockSpec((LANES * rows, LANES), lambda s: (s, 0)),
+        scratch_shapes=[pltpu.VMEM((rows * rows, LANES), F32)],
         compiler_params=pltpu.CompilerParams(vmem_limit_bytes=LIMIT),
         cost_estimate=pl.CostEstimate(flops=10**9, bytes_accessed=20 * 10**6, transcendentals=0),
         name="operators",
@@ -335,7 +391,7 @@
         compiler_params=pltpu.CompilerParams(vmem_limit_bytes=LIMIT),
         cost_estimate=pl.CostEstimate(flops=20 * 10**9, bytes_accessed=50 * 10**6, transcendentals=0),
         name="to_target",
-    )(me, source, multipoles, arrived, target_rows, weights, own, padded, place, octant.reshape(1, cells), l2l_ops)
+    )(me, source, multipoles, arrived, target_rows, weights, own, parent_locals, place, octant.reshape(1, cells), l2l_ops)
 
     return pl.pallas_call(
         lambda me, *refs: back_kernel(devices, reach, me, *refs),

time: 145 us -> 109 us (0.75)
  the two profiles are of different devices: /device:TPU:17 before, /device:TPU:0 now
where the time goes in v2:
time: 109 us; the launch traced here: 108 us
  Pallas kernels  80.8 us (74%)
  starting transfers between devices  15.3 us (14%)
  local copies, waits for them, and re-layouts  8.82 us (8%)
  waiting for transfers between devices  1.53 us (1%)
  other arithmetic  1.28 us (1%)
    pallas_call x1, Pallas kernels, shards(): pl.pallas_call(lambda *refs: target_kernel(devices, reach, slots, *refs[:...  33.1 us
    pallas_call x1, Pallas kernels, shards(): pl.pallas_call(lambda me, src, x, t, w, r, o, table, b0, b1, *accs: sourc...  30 us
    all_to_all x1, starting transfers between devices, shards(): arrived = lax.all_to_all(outgoing, axes, 0, 0, tiled=True)  8.79 us
    pallas_call x1, Pallas kernels, shards(): pl.pallas_call(ops_kernel, out_shape=jax.ShapeDtypeStruct((classes * rows...  8.1 us
    all_to_all x1, starting transfers between devices, shards(): back = lax.all_to_all(returned, axes, 0, 0, tiled=True)  6.55 us
    unnamed x22, local copies, waits for them, and re-layouts  5.45 us
    pallas_call x1, Pallas kernels, shards(): pl.pallas_call(lambda me, *refs: back_kernel(devices, reach, me, *refs),...  4.94 us
    pallas_call x1, Pallas kernels, shards(): pl.pallas_call(lambda me, *refs: export_kernel(me, devices, reach, *refs)...  4.78 us
  transfers between devices with their start and end apart: 2, of which 1 were waited for; matrix products, arithmetic and copies ran while one was open for 6% of the time, Pallas kernels for 66%

profile of v2, /device:TPU:0, one launch (start us, length us, event | category | flops | bytes accessed | tf_op | source)
XLA Modules:
  0.0 107.9 jit_solution(8047383515655418501)
XLA Ops:
  0.0 1.5 %copy.17.refs_2_.refs_7_ = f32[81,64]{1,0:T(8,128)} copy(f32[81,64]{0,1:T(8,128)} %param.11) | data formatting | bytes 41472 | tf_op args[1]
  1.5 1.3 %copy.24 = s32[1,26,128]{2,1,0:T(8,128)} copy(s32[1,26,128]{2,0,1:T(1,128)} %param.14) | data formatting | bytes 26624
  2.8 4.8 %exports.1 = f32[32,96,128]{2,1,0:T(8,128)} custom-call(s32[1]{0:T(128)} %bitcast.me.refs_0_, f32[81,512]{1,0:T(8,128)} %refs_2_.2, s32[26,128]{1,0:T(8,128)} %bitcast.8, f32[81,64]{1,0:T(8,128)} %copy.17.refs_2_.refs_7_), custom_call_target="tpu_custom_call" | custom-call | flops 1000000000 | bytes 2000000 | tf_op jit(solution)/shard_map/exports/pallas_call | solution.py:317
  7.6 8.8 %all-to-all-start = ((f32[32,96,128]{2,1,0:T(8,128)}), f32[32,96,128]{2,1,0:T(8,128)S(1)}, u32[]{:S(2)}, u32[]{:S(2)}) async-start(f32[32,96,128]{2,1,0:T(8,128)} %exports.1), calls=%async_computation | async-start | bytes 3145728 | tf_op jit(solution)/shard_map/all_to_all | solution.py:326
  16.4 0.5 broadcast.8
  16.9 0.7 reduce.3
  17.5 0.1 lt.13
  17.7 0.1 lt.14
  17.8 0.1 lt.15
  17.9 0.1 copy.18
  18.0 0.1 squeeze.7
  18.2 0.1 iota.12
  18.3 2.1 %copy.19.t = s32[16,256,4]{2,1,0:T(8,128)} copy(s32[16,256,4]{1,2,0:T(4,128)S(1)} %bitcast.7) | data formatting | bytes 131072 | tf_op jit(solution)/shard_map/transpose | solution.py:343
  20.4 0.1 copy.16
  20.5 0.7 reshape_squeeze.3.src.refs_1_
  21.2 8.1 %operators.1.w.refs_5_ = f32[22528,128]{1,0:T(8,128)} custom-call(f32[81,81,256]{2,1,0:T(8,128)} %m2l_ref.1), custom_call_target="tpu_custom_call" | custom-call | flops 1000000000 | bytes 20000000 | tf_op jit(solution)/shard_map/operators/pallas_call | solution.py:328
  29.3 30.0 %to_source.1 = (f32[32,88,128]{2,1,0:T(8,128)}, f32[512,128]{1,0:T(8,128)}) custom-call(s32[1]{0:T(128)} %bitcast.me.refs_0_, s32[16384]{0:T(1024)} %reshape_squeeze.3.src.refs_1_, f32[81,512]{1,0:T(8,128)} %refs_2_.2, s32[16,256,4]{2,1,0:T(8,128)} %copy.19.t, f32[22528,128]{1,0:T(8,128)} %operators.1.w.refs_5_), custom_call_target="tpu_custom_call" | custom-call | flops 20000000000 | bytes 50000000 | tf_op jit(solution)/shard_map/to_source/pallas_call | solution.py:348
  59.3 6.6 %all-to-all-start.1 = ((f32[32,88,128]{2,1,0:T(8,128)}), f32[32,88,128]{2,1,0:T(8,128)S(1)}, u32[]{:S(2)}, u32[]{:S(2)}) async-start(f32[32,88,128]{2,1,0:T(8,128)} %get-tuple-element.8), calls=%async_computation.1 | async-start | bytes 2883584 | tf_op jit(solution)/shard_map/all_to_all | solution.py:372
  65.9 0.8 copy.21.refs_10_
  66.7 0.6 subtract_add_fusion
  67.3 33.1 %to_target.1.refs_0_ = f32[81,512]{1,0:T(8,128)} custom-call(s32[1]{0:T(128)} %bitcast.me.refs_0_, s32[16384]{0:T(1024)} %reshape_squeeze.3.src.refs_1_, f32[81,512]{1,0:T(8,128)} %refs_2_.2, f32[32,96,128]{2,1,0:T(8,128)} %copy-done, s32[16,4,256]{2,1,0:T(4,128)} %copy-done.3, f32[22528,128]{1,0:T(8,128)} %operators.1.w.refs_5_, ...), custom_call_target="tpu_custom_call" | custom-call | flops 20000000000 | bytes 50000000 | tf_op jit(solution)/shard_map/to_target/pallas_call | solution.py:375
  100.3 1.5 %all-to-all-done.1.refs_1_ = f32[32,88,128]{2,1,0:T(8,128)S(1)} async-done(((f32[32,88,128]{2,1,0:T(8,128)}), f32[32,88,128]{2,1,0:T(8,128)S(1)}, u32[]{:S(2)}, u32[]{:S(2)}) %all-to-all-start.1) | async-done | bytes 1441824 | tf_op jit(solution)/shard_map/all_to_all | solution.py:372
  101.9 1.1 %copy-done.1 = f32[32,88,128]{2,1,0:T(8,128)} copy-done((f32[32,88,128]{2,1,0:T(8,128)}, f32[32,88,128]{2,1,0:T(8,128)S(1)}, u32[]{:S(2)}) %copy-start.1) | copy-done | bytes 1441816
  103.0 4.9 %returned.1 = f32[81,512]{1,0:T(8,128)} custom-call(s32[1]{0:T(128)} %bitcast.me.refs_0_, f32[81,512]{1,0:T(8,128)} %to_target.1.refs_0_, f32[32,88,128]{2,1,0:T(8,128)} %copy-done.1, s32[26,128]{1,0:T(8,128)} %bitcast.9), custom_call_target="tpu_custom_call" | custom-call | flops 1000000000 | bytes 2000000 | tf_op jit(solution)/shard_map/returned/pallas_call | solution.py:396
  (18 shorter events, 0.1 us)
Async XLA Ops:
  7.6 9.3 %copy-start.7 = (s32[1,256]{1,0:T(1,128)S(1)}, s32[1,256]{1,0:T(1,128)}, u32[]{:S(2)}) copy-start(s32[1,256]{1,0:T(1,128)} %param.17) | copy-start | bytes 3076
  7.6 10.4 %copy-start.4 = (s32[1,256,64]{1,2,0:T(8,128)S(1)}, s32[1,256,64]{1,2,0:T(8,128)}, u32[]{:S(2)}) copy-start(s32[1,256,64]{1,2,0:T(8,128)} %param.15) | copy-start | bytes 196612
  7.6 51.7 %all-to-all-start = ((f32[32,96,128]{2,1,0:T(8,128)}), f32[32,96,128]{2,1,0:T(8,128)S(1)}, u32[]{:S(2)}, u32[]{:S(2)}) async-start(f32[32,96,128]{2,1,0:T(8,128)} %exports.1), calls=%async_computation | async-start | bytes 3145728 | tf_op jit(solution)/shard_map/all_to_all | solution.py:326
  17.5 2.8 %copy-start.5 = (s32[1,256,64]{1,2,0:T(8,128)S(1)}, s32[1,256,64]{1,2,0:T(8,128)}, u32[]{:S(2)}) copy-start(s32[1,256,64]{1,2,0:T(8,128)} %param.16) | copy-start | bytes 196612
  18.3 11.0 %copy-start.3 = (s32[16,4,256]{2,1,0:T(4,128)}, s32[16,4,256]{2,1,0:T(4,128)S(1)}, u32[]{:S(2)}) copy-start(s32[16,4,256]{2,1,0:T(4,128)S(1)} %compare_select_fusion.refs_4_) | copy-start | bytes 196612
  59.3 6.6 %copy-start.2 = (f32[8,81,81]{2,0,1:T(8,128)S(1)}, f32[8,81,81]{2,0,1:T(8,128)}, u32[]{:S(2)}) copy-start(f32[8,81,81]{2,0,1:T(8,128)} %param.13) | copy-start | bytes 629860
  59.3 7.4 %copy-start = (f32[32,96,128]{2,1,0:T(8,128)}, f32[32,96,128]{2,1,0:T(8,128)S(1)}, u32[]{:S(2)}) copy-start(f32[32,96,128]{2,1,0:T(8,128)S(1)} %all-to-all-done.refs_3_) | copy-start | bytes 4718596
  59.3 7.4 %copy-start.6 = (s32[512]{0:T(512)S(1)}, s32[512]{0:T(512)}, u32[]{:S(2)}) copy-start(s32[512]{0:T(512)} %param.18) | copy-start | bytes 6148
  59.3 42.6 %all-to-all-start.1 = ((f32[32,88,128]{2,1,0:T(8,128)}), f32[32,88,128]{2,1,0:T(8,128)S(1)}, u32[]{:S(2)}, u32[]{:S(2)}) async-start(f32[32,88,128]{2,1,0:T(8,128)} %get-tuple-element.8), calls=%async_computation.1 | async-start | bytes 2883584 | tf_op jit(solution)/shard_map/all_to_all | solution.py:372
  101.9 1.1 %copy-start.1 = (f32[32,88,128]{2,1,0:T(8,128)}, f32[32,88,128]{2,1,0:T(8,128)S(1)}, u32[]{:S(2)}) copy-start(f32[32,88,128]{2,1,0:T(8,128)S(1)} %all-to-all-done.1.refs_1_) | copy-start | bytes 4325380

commit v3 on v2

--- a/solution.py
+++ b/solution.py
@@ -93,26 +93,34 @@
     return jnp.where(lax.broadcasted_iota(jnp.int32, rows.shape, 1) < coeffs, rows, 0.0)
 
 
+def peer_of(me, slot, reach, devices):
+    other = me[0] + peer_offset(slot, reach)
+    there = jnp.logical_and(other >= 0, other < devices)
+    return jnp.where(there, other, me[0]), there
+
+
 def export_kernel(me, devices, reach, x_ref, idx_ref, par_ref, out_ref):
     coeffs, cells = x_ref.shape
     rows = -(-coeffs // 8) * 8
-    high, low = split(pad_rows(x_ref[...], rows))
-    both = jnp.concatenate([high, low], axis=0)
+    both = jnp.concatenate(split(pad_rows(x_ref[...], rows)), axis=0)
     peers = idx_ref.shape[0]
-    parents = pad_rows(par_ref[...], LANES).T
+    room = jnp.zeros((HALO, LANES - coeffs), F32)
     line = lax.broadcasted_iota(jnp.int32, (cells, LANES), 0)
-    for slot in range(peers):
-        other = me[0] + peer_offset(slot, reach)
-
-        @pl.when(jnp.logical_and(other >= 0, other < devices))
-        def _():
-            hot = jnp.where(line == idx_ref[slot : slot + 1, :], 1.0, 0.0).astype(BF16)
-            sent = dot(both, hot)
-            out_ref[other, :rows] = sent[:rows] + sent[rows:]
-            if slot == reach - 1:
-                out_ref[other, coeffs : coeffs + HALO - 1] = halo_out(parents[:HALO], coeffs)
-            if slot == reach:
-                out_ref[other, coeffs : coeffs + HALO - 1] = halo_out(parents[-HALO:], coeffs)
+
+    def hot(slot):
+        return jnp.where(line == idx_ref[slot], 1.0, 0.0).astype(BF16)
+
+    for slot in range(0, peers, 2):
+        sent = dot(both, jnp.concatenate([hot(slot), hot(slot + 1)], axis=1))
+        sent = sent[:rows] + sent[rows:]
+        for k in range(2):
+            other, _ = peer_of(me, slot + k, reach, devices)
+            out_ref[other, :rows] = sent[:, k * LANES : (k + 1) * LANES]
+    total = par_ref.shape[0]
+    for slot, start in ((reach - 1, 0), (reach, total - HALO)):
+        other, _ = peer_of(me, slot, reach, devices)
+        parents = jnp.concatenate([par_ref[start : start + HALO, :], room], axis=1)
+        out_ref[other, coeffs : coeffs + HALO - 1] = halo_out(parents, coeffs)
 
 
 def ops_kernel(m2l_ref, out_ref, turned):
@@ -149,40 +157,53 @@
     )
 
 
-def source_kernel(devices, reach, slots, me, src, x_ref, tgt_ref, w_ref, ret_ref, own_ref, table, bufs, accs):
+def source_kernel(devices, reach, steps_total, me, src, x_ref, tgt_ref, cnt_ref, w_ref, ret_ref, own_ref, table, lists, bufs, accs):
     step = pl.program_id(0)
     steps = pl.num_programs(0)
     coeffs, cells = x_ref.shape
-    groups = tgt_ref.shape[2]
-    classes = GROUP // slots
-    pitch = w_ref.shape[0] // (groups * classes)
+    slots, classes = tgt_ref.shape
+    block = classes // steps
+    per = GROUP // slots
+    groups = block // per
+    pitch = w_ref.shape[0] // block
 
     @pl.when(step == 0)
     def _():
         sign = parity_at(lax.broadcasted_iota(jnp.int32, (coeffs, cells), 0))
         table[...] = stacked(x_ref[...] * sign, coeffs).T.astype(BF16)
+        slot = lax.broadcasted_iota(jnp.int32, (slots, classes), 0)
+        live = jnp.where(slot < cnt_ref[...], tgt_ref[...], -1)
+        for k in range(steps_total):
+            lists[k, :, :block] = live[:, k * block : (k + 1) * block]
         for acc in accs:
             acc[...] = jnp.zeros_like(acc)
 
-    line = lax.broadcasted_iota(jnp.int32, (GROUP, cells), 1)
+    line = lax.broadcasted_iota(jnp.int32, (slots, cells), 1)
+    listed = lists[step]
 
     def compute(g):
-        hot = jnp.where(tgt_ref[0, :, g : g + 1] == line, 1.0, 0.0).astype(BF16)
+        hot = jnp.concatenate(
+            [
+                jnp.where(listed[:, k : k + 1] == line, 1.0, 0.0).astype(BF16)
+                for k in range(g * per, (g + 1) * per)
+            ],
+            axis=0,
+        )
         columns = dot(hot, table[...]).astype(BF16)
-        bufs[g % 2][...] = products(columns, w_ref, g * classes, pitch, slots, coeffs)
+        bufs[g % 2][...] = products(columns, w_ref, g * per, pitch, slots, coeffs)
 
     def scatter(buf, base):
         for q in range(GROUP):
             acc = accs[q % len(accs)]
-            row = src[base + q]
+            row = src[q % slots, base + q // slots]
             acc[pl.ds(row, 1), :] += buf[q : q + 1, :]
 
-    base = step * (groups * GROUP)
+    base = step * block
     compute(0)
     for g in range(1, groups):
         compute(g)
-        scatter(bufs[(g - 1) % 2], base + (g - 1) * GROUP)
-    scatter(bufs[(groups - 1) % 2], base + (groups - 1) * GROUP)
+        scatter(bufs[(g - 1) % 2], base + (g - 1) * per)
+    scatter(bufs[(groups - 1) % 2], base + (groups - 1) * per)
 
     @pl.when(step == steps - 1)
     def _():
@@ -198,11 +219,8 @@
             own_ref[start : start + LANES, :] = total(start)
         rows = ret_ref.shape[1]
         for slot in range((accs[0].shape[0] - cells) // LANES):
-            other = me[0] + peer_offset(slot, reach)
-
-            @pl.when(jnp.logical_and(other >= 0, other < devices))
-            def _():
-                ret_ref[other] = total(cells + slot * LANES).T[:rows]
+            other, _ = peer_of(me, slot, reach, devices)
+            ret_ref[other] = total(cells + slot * LANES).T[:rows]
 
 
 def target_kernel(
@@ -220,7 +238,7 @@
     def _():
         table[:cells, :] = tagged(x_ref[...], coeffs).T
         for slot in range((table.shape[0] - cells) // LANES):
-            other = jnp.clip(me[0] + peer_offset(slot, reach), 0, devices - 1)
+            other, _ = peer_of(me, slot, reach, devices)
             start = cells + slot * LANES
             table[start : start + LANES, :] = tagged(got_ref[other, :coeffs], coeffs).T
         near[...] = jnp.zeros_like(near)
@@ -229,23 +247,24 @@
 
     def gather(buf, base):
         for q in range(GROUP):
-            buf[q : q + 1, :] = table[pl.ds(src[base + q], 1), :]
+            buf[q : q + 1, :] = table[pl.ds(src[q % slots, base + q // slots], 1), :]
 
     def compute(g):
         y = products(paired(bufs[g % 2][...], coeffs), w_ref, g * classes, pitch, slots, coeffs)
         hot = jnp.where(tgt_ref[0, g : g + 1, :] == line, 1.0, 0.0).astype(BF16)
         near[...] += dot(hot, jnp.concatenate(split(y), axis=1))
 
-    base = step * (groups * GROUP)
+    base = step * groups * classes
     gather(bufs[0], base)
     for g in range(groups):
         if g + 1 < groups:
-            gather(bufs[(g + 1) % 2], base + (g + 1) * GROUP)
+            gather(bufs[(g + 1) % 2], base + (g + 1) * classes)
         compute(g)
 
     @pl.when(step == steps - 1)
     def _():
-        parts = [None, pad_rows(par_ref[...], LANES).T, None]
+        room = jnp.zeros((par_ref.shape[0], LANES - coeffs), F32)
+        parts = [None, jnp.concatenate([par_ref[...], room], axis=1), None]
         for part, shift in ((0, -1), (2, 1)):
             other = jnp.clip(me[0] + shift, 0, devices - 1)
             sent = halo_in(got_ref[other, coeffs : coeffs + HALO - 1], coeffs)
@@ -269,20 +288,19 @@
         out_ref[...] = total
 
 
-def back_kernel(devices, reach, me, base_ref, got_ref, idx_ref, out_ref, total):
+def back_kernel(devices, reach, me, base_ref, got_ref, idx_ref, out_ref):
     coeffs, cells = base_ref.shape
     rows = got_ref.shape[1]
-    total[...] = jnp.zeros_like(total)
     line = lax.broadcasted_iota(jnp.int32, (cells, LANES), 0)
-    for slot in range(idx_ref.shape[0]):
-        other = me[0] + peer_offset(slot, reach)
-
-        @pl.when(jnp.logical_and(other >= 0, other < devices))
-        def _():
-            hot = jnp.where(line == idx_ref[slot : slot + 1, :], 1.0, 0.0).astype(BF16)
-            both = jnp.concatenate(split(got_ref[other]), axis=0)
-            total[...] += dot_nt(both, hot)
-
+    total = jnp.zeros((2 * rows, cells), F32)
+    for slot in range(0, idx_ref.shape[0], 2):
+        hots, gots = [], []
+        for k in (slot, slot + 1):
+            other, there = peer_of(me, k, reach, devices)
+            place = jnp.where(there, idx_ref[k], -1)
+            hots.append(jnp.where(line == place, 1.0, 0.0).astype(BF16))
+            gots.append(jnp.concatenate(split(got_ref[other]), axis=0))
+        total = total + dot_nt(jnp.concatenate(gots, axis=1), jnp.concatenate(hots, axis=1))
     out_ref[...] = base_ref[...] + total[:coeffs] + total[rows : rows + coeffs]
 
 
@@ -302,8 +320,9 @@
 ):
     axes = ("gx", "gy")
     coeffs, cells = multipoles.shape
-    exported = export_cells[0]
-    peers, send = exported.shape
+    exported = jnp.transpose(export_cells, (1, 0, 2))
+    peers, _, send = exported.shape
+    parents = parent_locals.T
     reach = peers // 2
     classes = m2l_ops.shape[2]
     slots = pair_first.shape[2]
@@ -311,7 +330,7 @@
     position = lax.axis_index("gx") * lax.axis_size("gy") + lax.axis_index("gy")
     me = position.reshape(1).astype(jnp.int32)
     rows = -(-coeffs // 8) * 8
-    steps = 16
+    steps = 4
     groups = classes * slots // (GROUP * steps)
 
     outgoing = pl.pallas_call(
@@ -322,7 +341,7 @@
         compiler_params=pltpu.CompilerParams(vmem_limit_bytes=LIMIT),
         cost_estimate=pl.CostEstimate(flops=10**9, bytes_accessed=2 * 10**6, transcendentals=0),
         name="exports",
-    )(me, multipoles, exported, parent_locals)
+    )(me, multipoles, exported, parents)
     arrived = lax.all_to_all(outgoing, axes, 0, 0, tiled=True)
 
     weights = pl.pallas_call(
@@ -337,17 +356,12 @@
         name="operators",
     )(m2l_ops)
 
-    live = lax.broadcasted_iota(jnp.int32, (classes, slots), 1) < pair_count[0][:, None]
-    target = jnp.where(live, pair_first[0], -1)
-    target_rows = target.reshape(steps, groups, GROUP)
-    target_columns = jnp.transpose(target_rows, (0, 2, 1))
-    source = pair_second[0].reshape(-1)
-
+    source = pair_second[0].T
     w_spec = pl.BlockSpec((groups * GROUP // slots * rows, LANES), lambda s, *_: (s, 0))
     whole = pl.BlockSpec(memory_space=pltpu.VMEM)
     returned, own = pl.pallas_call(
-        lambda me, src, x, t, w, r, o, table, b0, b1, *accs: source_kernel(
-            devices, reach, slots, me, src, x, t, w, r, o, table, (b0, b1), accs
+        lambda me, src, x, t, n, w, r, o, table, lists, b0, b1, *accs: source_kernel(
+            devices, reach, steps, me, src, x, t, n, w, r, o, table, lists, (b0, b1), accs
         ),
         out_shape=(
             jax.ShapeDtypeStruct((devices, rows, send), F32),
@@ -356,10 +370,11 @@
         grid_spec=pltpu.PrefetchScalarGridSpec(
             num_scalar_prefetch=2,
             grid=(steps,),
-            in_specs=[whole, pl.BlockSpec((1, GROUP, groups), lambda s, *_: (s, 0, 0)), w_spec],
+            in_specs=[whole, whole, whole, w_spec],
             out_specs=(whole, whole),
             scratch_shapes=[
                 pltpu.VMEM((cells, 2 * LANES), BF16),
+                pltpu.VMEM((steps, slots, -(-classes // steps // LANES) * LANES), jnp.int32),
                 pltpu.VMEM((GROUP, LANES), F32),
                 pltpu.VMEM((GROUP, LANES), F32),
             ]
@@ -368,9 +383,12 @@
         compiler_params=pltpu.CompilerParams(vmem_limit_bytes=LIMIT),
         cost_estimate=pl.CostEstimate(flops=20 * 10**9, bytes_accessed=50 * 10**6, transcendentals=0),
         name="to_source",
-    )(me, source, multipoles, target_columns, weights)
+    )(me, source, multipoles, pair_first[0].T, pair_count, weights)
     back = lax.all_to_all(returned, axes, 0, 0, tiled=True)
 
+    own, pair_first, pair_count = lax.optimization_barrier((own, pair_first, pair_count))
+    live = lax.broadcasted_iota(jnp.int32, (classes, slots), 1) < pair_count[0][:, None]
+    target_rows = jnp.where(live, pair_first[0], -1).reshape(steps, groups, GROUP)
     place = (parent_of - position * parent_locals.shape[1] + HALO).reshape(1, cells)
     base = pl.pallas_call(
         lambda *refs: target_kernel(devices, reach, slots, *refs[:14], refs[14:]),
@@ -391,15 +409,14 @@
         compiler_params=pltpu.CompilerParams(vmem_limit_bytes=LIMIT),
         cost_estimate=pl.CostEstimate(flops=20 * 10**9, bytes_accessed=50 * 10**6, transcendentals=0),
         name="to_target",
-    )(me, source, multipoles, arrived, target_rows, weights, own, parent_locals, place, octant.reshape(1, cells), l2l_ops)
+    )(me, source, multipoles, arrived, target_rows, weights, own, parents, place, octant.reshape(1, cells), l2l_ops)
 
     return pl.pallas_call(
         lambda me, *refs: back_kernel(devices, reach, me, *refs),
         out_shape=jax.ShapeDtypeStruct((coeffs, cells), F32),
         in_specs=[smem(), vmem(), vmem(), vmem()],
         out_specs=vmem(),
-        scratch_shapes=[pltpu.VMEM((2 * rows, cells), F32)],
-        compiler_params=pltpu.CompilerParams(vmem_limit_bytes=LIMIT),
+        compiler_params=pltpu.CompilerParams(vmem_limit_bytes=LIMIT // 4),
         cost_estimate=pl.CostEstimate(flops=10**9, bytes_accessed=2 * 10**6, transcendentals=0),
         name="returned",
     )(me, base, back, exported)

time: 109 us -> 91.4 us (0.84)
  Pallas kernels: 80.8 us -> 66.6 us
  waiting for transfers between devices: 1.53 us -> 9.11 us
  local copies, waits for them, and re-layouts: 8.82 us -> 2.93 us
  starting transfers between devices: 15.3 us -> 10.3 us
    all_to_all x1, waiting for transfers between devices: 0.01 us -> 5.75 us  [shards(): arrived = lax.all_to_all(outgoing, axes, 0, 0, tiled=True)]
    pallas_call x1, Pallas kernels: 30 us -> 25 us  [shards(): pl.pallas_call(lambda me, src, x, t, n, w, r, o, table, lists, b0, b1, *a...]
    pallas_call x1, Pallas kernels: 33.1 us -> 28.6 us  [shards(): pl.pallas_call(lambda *refs: target_kernel(devices, reach, slots, *refs[:...]
    unnamed x22 -> x15, local copies, waits for them, and re-layouts: 5.45 us -> 1.77 us
    all_to_all x1, starting transfers between devices: 6.55 us -> 3.01 us  [shards(): back = lax.all_to_all(returned, axes, 0, 0, tiled=True)]
    pallas_call x1, Pallas kernels: 4.94 us -> 1.96 us  [shards(): pl.pallas_call(lambda me, *refs: back_kernel(devices, reach, me, *refs),...]
    transpose x1 -> x0, local copies, waits for them, and re-layouts: 2.09 us -> none  [shards(): target_columns = jnp.transpose(target_rows, (0, 2, 1))]
    all_to_all x1, waiting for transfers between devices: 1.53 us -> 3.36 us  [shards(): back = lax.all_to_all(returned, axes, 0, 0, tiled=True)]
  transfers between devices with their start and end apart: 2 -> 2, of which waited for: 1 -> 2; matrix products, arithmetic and copies ran while one was open for 6% -> 4% of each run, Pallas kernels for 66% -> 68%
where the time goes in v3:
time: 91.4 us; the launch traced here: 90.9 us
  Pallas kernels  66.6 us (73%)
  starting transfers between devices  10.3 us (11%)
  waiting for transfers between devices  9.11 us (10%)
  local copies, waits for them, and re-layouts  2.93 us (3%)
  other arithmetic  1.87 us (2%)
    pallas_call x1, Pallas kernels, shards(): pl.pallas_call(lambda *refs: target_kernel(devices, reach, slots, *refs[:...  28.6 us
    pallas_call x1, Pallas kernels, shards(): pl.pallas_call(lambda me, src, x, t, n, w, r, o, table, lists, b0, b1, *a...  25 us
    pallas_call x1, Pallas kernels, shards(): pl.pallas_call(ops_kernel, out_shape=jax.ShapeDtypeStruct((classes * rows...  8.11 us
    all_to_all x1, starting transfers between devices, shards(): arrived = lax.all_to_all(outgoing, axes, 0, 0, tiled=True)  7.3 us
    all_to_all x1, waiting for transfers between devices, shards(): arrived = lax.all_to_all(outgoing, axes, 0, 0, tiled=True)  5.75 us
    all_to_all x1, waiting for transfers between devices, shards(): back = lax.all_to_all(returned, axes, 0, 0, tiled=True)  3.36 us
    pallas_call x1, Pallas kernels, shards(): pl.pallas_call(lambda me, *refs: export_kernel(me, devices, reach, *refs)...  3.03 us
    all_to_all x1, starting transfers between devices, shards(): back = lax.all_to_all(returned, axes, 0, 0, tiled=True)  3.01 us
  transfers between devices with their start and end apart: 2, of which 2 were waited for; matrix products, arithmetic and copies ran while one was open for 4% of the time, Pallas kernels for 68%

profile of v3, /device:TPU:0, one launch (start us, length us, event | category | flops | bytes accessed | tf_op | source)
XLA Modules:
  0.0 90.9 jit_solution(13957918996907627734)
XLA Ops:
  0.0 3.0 %exports.1 = f32[32,96,128]{2,1,0:T(8,128)} custom-call(s32[1]{0:T(128)} %bitcast.me.refs_0_, f32[81,512]{1,0:T(8,128)} %refs_2_.1, s32[26,1,128]{2,1,0:T(1,128)} %bitcast.11, f32[64,81]{1,0:T(8,128)} %bitcast.17), custom_call_target="tpu_custom_call" | custom-call | flops 1000000000 | bytes 2000000 | tf_op jit(solution)/shard_map/exports/pallas_call | solution.py:336
  3.0 7.3 %all-to-all-start = ((f32[32,96,128]{2,1,0:T(8,128)}), f32[32,96,128]{2,1,0:T(8,128)S(1)}, u32[]{:S(2)}, u32[]{:S(2)}) async-start(f32[32,96,128]{2,1,0:T(8,128)} %exports.1), calls=%async_computation | async-start | bytes 3145728 | tf_op jit(solution)/shard_map/all_to_all | solution.py:345
  10.3 8.1 %operators.1.w.refs_5_ = f32[22528,128]{1,0:T(8,128)} custom-call(f32[81,81,256]{2,1,0:T(8,128)} %m2l_ref.1), custom_call_target="tpu_custom_call" | custom-call | flops 1000000000 | bytes 20000000 | tf_op jit(solution)/shard_map/operators/pallas_call | solution.py:347
  18.4 25.0 %to_source.1 = (f32[32,88,128]{2,1,0:T(8,128)}, f32[512,128]{1,0:T(8,128)}) custom-call(s32[1]{0:T(128)} %bitcast.me.refs_0_, s32[64,256]{1,0:T(8,128)} %bitcast.15, f32[81,512]{1,0:T(8,128)} %refs_2_.1, s32[64,256]{1,0:T(8,128)} %bitcast.13, s32[1,256]{1,0:T(1,128)} %n.1, f32[22528,128]{1,0:T(8,128)} %operators.1.w.refs_5_), custom_call_target="tpu_custom_call" | custom-call | flops 20000000000 | bytes 50000000 | tf_op jit(solution)/shard_map/to_source/pallas_call | solution.py:362
  43.4 5.8 %all-to-all-done.refs_3_ = f32[32,96,128]{2,1,0:T(8,128)S(1)} async-done(((f32[32,96,128]{2,1,0:T(8,128)}), f32[32,96,128]{2,1,0:T(8,128)S(1)}, u32[]{:S(2)}, u32[]{:S(2)}) %all-to-all-start) | async-done | bytes 1572896 | tf_op jit(solution)/shard_map/all_to_all | solution.py:345
  49.2 3.0 %all-to-all-start.1 = ((f32[32,88,128]{2,1,0:T(8,128)}), f32[32,88,128]{2,1,0:T(8,128)S(1)}, u32[]{:S(2)}, u32[]{:S(2)}) async-start(f32[32,88,128]{2,1,0:T(8,128)} %get-tuple-element.14), calls=%async_computation.1 | async-start | bytes 2883584 | tf_op jit(solution)/shard_map/all_to_all | solution.py:387
  52.2 0.0 copy-done.4
  52.2 0.1 copy.13
  52.3 0.1 squeeze.11
  52.4 0.5 broadcast.8
  52.9 0.0 copy-done.6
  52.9 0.7 reduce.3
  53.6 0.1 lt.13
  53.7 0.1 lt.14
  53.8 0.1 lt.15
  54.0 0.1 iota.12
  54.0 0.0 copy-done.3
  54.0 0.8 copy.14.refs_10_
  54.9 0.6 subtract_add_fusion
  55.5 0.6 compare_select_fusion.refs_4_
  56.1 28.6 %to_target.1.refs_0_ = f32[81,512]{1,0:T(8,128)} custom-call(s32[1]{0:T(128)} %bitcast.me.refs_0_, s32[64,256]{1,0:T(8,128)} %bitcast.16, f32[81,512]{1,0:T(8,128)} %refs_2_.1, f32[32,96,128]{2,1,0:T(8,128)} %copy-done.2, s32[4,16,256]{2,1,0:T(8,128)} %compare_select_fusion.refs_4_, f32[22528,128]{1,0:T(8,128)} %operators.1.w.refs_5_, ...), custom_call_target="tpu_custom_call" | custom-call | flops 20000000000 | bytes 50000000 | tf_op jit(solution)/shard_map/to_target/pallas_call | solution.py:393
  84.7 3.4 %all-to-all-done.1.refs_1_ = f32[32,88,128]{2,1,0:T(8,128)S(1)} async-done(((f32[32,88,128]{2,1,0:T(8,128)}), f32[32,88,128]{2,1,0:T(8,128)S(1)}, u32[]{:S(2)}, u32[]{:S(2)}) %all-to-all-start.1) | async-done | bytes 1441824 | tf_op jit(solution)/shard_map/all_to_all | solution.py:387
  88.0 0.9 %copy-done.1 = f32[81,512]{1,0:T(8,128)S(1)} copy-done((f32[81,512]{1,0:T(8,128)S(1)}, f32[81,512]{1,0:T(8,128)}, u32[]{:S(2)}) %copy-start.1) | copy-done | bytes 165912
  88.9 2.0 %returned.1 = f32[81,512]{1,0:T(8,128)} custom-call(s32[1]{0:T(128)} %bitcast.me.refs_0_, f32[81,512]{1,0:T(8,128)S(1)} %copy-done.1, f32[32,88,128]{2,1,0:T(8,128)S(1)} %all-to-all-done.1.refs_1_, s32[26,1,128]{2,1,0:T(1,128)S(1)} %bitcast.12), custom_call_target="tpu_custom_call" | custom-call | flops 1000000000 | bytes 2000000 | tf_op jit(solution)/shard_map/returned/pallas_call | solution.py:414
  (11 shorter events, 0.0 us)
Async XLA Ops:
  3.0 46.1 %all-to-all-start = ((f32[32,96,128]{2,1,0:T(8,128)}), f32[32,96,128]{2,1,0:T(8,128)S(1)}, u32[]{:S(2)}, u32[]{:S(2)}) async-start(f32[32,96,128]{2,1,0:T(8,128)} %exports.1), calls=%async_computation | async-start | bytes 3145728 | tf_op jit(solution)/shard_map/all_to_all | solution.py:345
  43.4 8.8 %copy-start.4 = (s32[1,256,64]{1,2,0:T(8,128)S(1)}, s32[1,256,64]{1,2,0:T(8,128)}, u32[]{:S(2)}) copy-start(s32[1,256,64]{1,2,0:T(8,128)} %param.15) | copy-start | bytes 196612
  49.2 3.2 %copy-start.2 = (f32[32,96,128]{2,1,0:T(8,128)}, f32[32,96,128]{2,1,0:T(8,128)S(1)}, u32[]{:S(2)}) copy-start(f32[32,96,128]{2,1,0:T(8,128)S(1)} %all-to-all-done.refs_3_) | copy-start | bytes 4718596
  49.2 3.7 %copy-start.6 = (s32[1,256]{1,0:T(1,128)S(1)}, s32[1,256]{1,0:T(1,128)}, u32[]{:S(2)}) copy-start(s32[1,256]{1,0:T(1,128)} %n.1) | copy-start | bytes 3076
  49.2 4.9 %copy-start.3 = (f32[8,81,81]{2,0,1:T(8,128)S(1)}, f32[8,81,81]{2,0,1:T(8,128)}, u32[]{:S(2)}) copy-start(f32[8,81,81]{2,0,1:T(8,128)} %param.13) | copy-start | bytes 629860
  49.2 5.7 %copy-start.5 = (s32[512]{0:T(512)S(1)}, s32[512]{0:T(512)}, u32[]{:S(2)}) copy-start(s32[512]{0:T(512)} %param.18) | copy-start | bytes 6148
  49.2 38.8 %all-to-all-start.1 = ((f32[32,88,128]{2,1,0:T(8,128)}), f32[32,88,128]{2,1,0:T(8,128)S(1)}, u32[]{:S(2)}, u32[]{:S(2)}) async-start(f32[32,88,128]{2,1,0:T(8,128)} %get-tuple-element.14), calls=%async_computation.1 | async-start | bytes 2883584 | tf_op jit(solution)/shard_map/all_to_all | solution.py:387
  56.1 31.9 %copy-start = (s32[1,26,128]{2,0,1:T(1,128)S(1)}, s32[1,26,128]{2,0,1:T(1,128)}, u32[]{:S(2)}) copy-start(s32[1,26,128]{2,0,1:T(1,128)} %param.14) | copy-start | bytes 39940
  88.0 0.9 %copy-start.1 = (f32[81,512]{1,0:T(8,128)S(1)}, f32[81,512]{1,0:T(8,128)}, u32[]{:S(2)}) copy-start(f32[81,512]{1,0:T(8,128)} %to_target.1.refs_0_) | copy-start | bytes 497668

commit v4 on v3

--- a/solution.py
+++ b/solution.py
@@ -74,22 +74,34 @@
     return jnp.concatenate([left, right], axis=1).astype(BF16)
 
 
+def halo_rows(coeffs):
+    return -(-HALO * coeffs // LANES)
+
+
 def halo_out(rows, coeffs):
     lane = lax.broadcasted_iota(jnp.int32, (1, LANES), 1)
-    room = LANES - coeffs
-    last = rows[HALO - 1 :]
-    first = jnp.where(lane < coeffs, rows[:1], pltpu.roll(last, coeffs, 1))
-    second = jnp.where(lane < coeffs, rows[1:2], pltpu.roll(last, coeffs - room, 1))
-    return jnp.concatenate([first, second, rows[2 : HALO - 1]], axis=0)
+    room, kept = LANES - coeffs, halo_rows(coeffs)
+    spare = []
+    for k in range(kept, HALO):
+        for start in range(0, coeffs, room):
+            spare.append(pltpu.roll(rows[k : k + 1], (coeffs - start) % LANES, 1))
+    spare += [jnp.zeros((1, LANES), F32)] * (kept - len(spare))
+    spare = jnp.concatenate(spare, axis=0)
+    return jnp.where(lane < coeffs, rows[:kept], spare)
 
 
 def halo_in(sent, coeffs):
     lane = lax.broadcasted_iota(jnp.int32, (1, LANES), 1)
-    room = LANES - coeffs
-    last = jnp.where(
-        lane < room, pltpu.roll(sent[:1], room, 1), pltpu.roll(sent[1:2], LANES + room - coeffs, 1)
-    )
-    rows = jnp.concatenate([sent, last], axis=0)
+    room, kept = LANES - coeffs, halo_rows(coeffs)
+    rows, at = [sent], 0
+    for k in range(kept, HALO):
+        row = jnp.zeros((1, LANES), F32)
+        for start in range(0, coeffs, room):
+            piece = pltpu.roll(sent[at : at + 1], (start - coeffs) % LANES, 1)
+            row = jnp.where(jnp.logical_and(lane >= start, lane < start + room), piece, row)
+            at += 1
+        rows.append(row)
+    rows = jnp.concatenate(rows, axis=0)
     return jnp.where(lax.broadcasted_iota(jnp.int32, rows.shape, 1) < coeffs, rows, 0.0)
 
 
@@ -104,6 +116,7 @@
     rows = -(-coeffs // 8) * 8
     both = jnp.concatenate(split(pad_rows(x_ref[...], rows)), axis=0)
     peers = idx_ref.shape[0]
+    held = out_ref.shape[0] // devices
     room = jnp.zeros((HALO, LANES - coeffs), F32)
     line = lax.broadcasted_iota(jnp.int32, (cells, LANES), 0)
 
@@ -115,12 +128,12 @@
         sent = sent[:rows] + sent[rows:]
         for k in range(2):
             other, _ = peer_of(me, slot + k, reach, devices)
-            out_ref[other, :rows] = sent[:, k * LANES : (k + 1) * LANES]
+            out_ref[pl.ds(other * held, coeffs), :] = sent[:coeffs, k * LANES : (k + 1) * LANES]
     total = par_ref.shape[0]
     for slot, start in ((reach - 1, 0), (reach, total - HALO)):
         other, _ = peer_of(me, slot, reach, devices)
         parents = jnp.concatenate([par_ref[start : start + HALO, :], room], axis=1)
-        out_ref[other, coeffs : coeffs + HALO - 1] = halo_out(parents, coeffs)
+        out_ref[pl.ds(other * held + coeffs, held - coeffs), :] = halo_out(parents, coeffs)
 
 
 def ops_kernel(m2l_ref, out_ref, turned):
@@ -157,7 +170,7 @@
     )
 
 
-def source_kernel(devices, reach, steps_total, me, src, x_ref, tgt_ref, cnt_ref, w_ref, ret_ref, own_ref, table, lists, bufs, accs):
+def source_kernel(devices, reach, steps_total, me, src, x_ref, tgt_ref, cnt_ref, w_ref, ret_ref, own_ref, live_ref, table, lists, bufs, accs):
     step = pl.program_id(0)
     steps = pl.num_programs(0)
     coeffs, cells = x_ref.shape
@@ -173,6 +186,7 @@
         table[...] = stacked(x_ref[...] * sign, coeffs).T.astype(BF16)
         slot = lax.broadcasted_iota(jnp.int32, (slots, classes), 0)
         live = jnp.where(slot < cnt_ref[...], tgt_ref[...], -1)
+        live_ref[...] = live.T
         for k in range(steps_total):
             lists[k, :, :block] = live[:, k * block : (k + 1) * block]
         for acc in accs:
@@ -217,10 +231,9 @@
 
         for start in range(0, cells, LANES):
             own_ref[start : start + LANES, :] = total(start)
-        rows = ret_ref.shape[1]
         for slot in range((accs[0].shape[0] - cells) // LANES):
             other, _ = peer_of(me, slot, reach, devices)
-            ret_ref[other] = total(cells + slot * LANES).T[:rows]
+            ret_ref[pl.ds(other * coeffs, coeffs), :] = total(cells + slot * LANES).T[:coeffs]
 
 
 def target_kernel(
@@ -230,6 +243,7 @@
     step = pl.program_id(0)
     steps = pl.num_programs(0)
     coeffs, cells = x_ref.shape
+    held = got_ref.shape[0] // devices
     groups = tgt_ref.shape[1]
     classes = GROUP // slots
     pitch = w_ref.shape[0] // (groups * classes)
@@ -240,7 +254,7 @@
         for slot in range((table.shape[0] - cells) // LANES):
             other, _ = peer_of(me, slot, reach, devices)
             start = cells + slot * LANES
-            table[start : start + LANES, :] = tagged(got_ref[other, :coeffs], coeffs).T
+            table[start : start + LANES, :] = tagged(got_ref[pl.ds(other * held, coeffs), :], coeffs).T
         near[...] = jnp.zeros_like(near)
 
     line = lax.broadcasted_iota(jnp.int32, (cells, GROUP), 0)
@@ -267,13 +281,13 @@
         parts = [None, jnp.concatenate([par_ref[...], room], axis=1), None]
         for part, shift in ((0, -1), (2, 1)):
             other = jnp.clip(me[0] + shift, 0, devices - 1)
-            sent = halo_in(got_ref[other, coeffs : coeffs + HALO - 1], coeffs)
+            sent = halo_in(got_ref[pl.ds(other * held + coeffs, held - coeffs), :], coeffs)
             parts[part] = jnp.where(other == me[0], 0.0, sent)
         parents = jnp.concatenate(parts, axis=0)
         wide = parents.shape[0]
         parents = jnp.concatenate(split(parents.T), axis=0)
         hot = jnp.where(
-            pos_ref[...] == lax.broadcasted_iota(jnp.int32, (wide, cells), 0), 1.0, 0.0
+            pos_ref[...] - (me[0] * par_ref.shape[0] - HALO) == lax.broadcasted_iota(jnp.int32, (wide, cells), 0), 1.0, 0.0
         ).astype(BF16)
         picked = dot(parents, hot).astype(BF16)
         total = (near[:, :LANES] + near[:, LANES:] + own_ref[...]).T[:coeffs]
@@ -288,18 +302,22 @@
         out_ref[...] = total
 
 
-def back_kernel(devices, reach, me, base_ref, got_ref, idx_ref, out_ref):
+def back_kernel(devices, reach, me, base_ref, got_any, idx_ref, out_ref, got_ref, done):
     coeffs, cells = base_ref.shape
-    rows = got_ref.shape[1]
+    rows = -(-coeffs // 8) * 8
+    copy = pltpu.make_async_copy(got_any, got_ref, done)
+    copy.start()
     line = lax.broadcasted_iota(jnp.int32, (cells, LANES), 0)
     total = jnp.zeros((2 * rows, cells), F32)
+    copy.wait()
     for slot in range(0, idx_ref.shape[0], 2):
         hots, gots = [], []
         for k in (slot, slot + 1):
             other, there = peer_of(me, k, reach, devices)
             place = jnp.where(there, idx_ref[k], -1)
             hots.append(jnp.where(line == place, 1.0, 0.0).astype(BF16))
-            gots.append(jnp.concatenate(split(got_ref[other]), axis=0))
+            got = pad_rows(got_ref[pl.ds(other * coeffs, coeffs), :], rows)
+            gots.append(jnp.concatenate(split(got), axis=0))
         total = total + dot_nt(jnp.concatenate(gots, axis=1), jnp.concatenate(hots, axis=1))
     out_ref[...] = base_ref[...] + total[:coeffs] + total[rows : rows + coeffs]
 
@@ -333,16 +351,23 @@
     steps = 4
     groups = classes * slots // (GROUP * steps)
 
+    held = coeffs + halo_rows(coeffs)
+
+    def exchange(blocks):
+        lines = blocks.shape[0] // devices
+        cut = blocks.reshape(devices, lines, 1, send)
+        return lax.all_to_all(cut, axes, 0, 0, tiled=True).reshape(blocks.shape)
+
     outgoing = pl.pallas_call(
         lambda me, *refs: export_kernel(me, devices, reach, *refs),
-        out_shape=jax.ShapeDtypeStruct((devices, coeffs + HALO - 1, send), F32),
+        out_shape=jax.ShapeDtypeStruct((devices * held, send), F32),
         in_specs=[smem(), vmem(), vmem(), vmem()],
         out_specs=vmem(),
         compiler_params=pltpu.CompilerParams(vmem_limit_bytes=LIMIT),
         cost_estimate=pl.CostEstimate(flops=10**9, bytes_accessed=2 * 10**6, transcendentals=0),
         name="exports",
     )(me, multipoles, exported, parents)
-    arrived = lax.all_to_all(outgoing, axes, 0, 0, tiled=True)
+    arrived = exchange(outgoing)
 
     weights = pl.pallas_call(
         ops_kernel,
@@ -359,19 +384,20 @@
     source = pair_second[0].T
     w_spec = pl.BlockSpec((groups * GROUP // slots * rows, LANES), lambda s, *_: (s, 0))
     whole = pl.BlockSpec(memory_space=pltpu.VMEM)
-    returned, own = pl.pallas_call(
-        lambda me, src, x, t, n, w, r, o, table, lists, b0, b1, *accs: source_kernel(
-            devices, reach, steps, me, src, x, t, n, w, r, o, table, lists, (b0, b1), accs
+    returned, own, live = pl.pallas_call(
+        lambda me, src, x, t, n, w, r, o, v, table, lists, b0, b1, *accs: source_kernel(
+            devices, reach, steps, me, src, x, t, n, w, r, o, v, table, lists, (b0, b1), accs
         ),
         out_shape=(
-            jax.ShapeDtypeStruct((devices, rows, send), F32),
+            jax.ShapeDtypeStruct((devices * coeffs, send), F32),
             jax.ShapeDtypeStruct((cells, LANES), F32),
+            jax.ShapeDtypeStruct((classes, slots), jnp.int32),
         ),
         grid_spec=pltpu.PrefetchScalarGridSpec(
             num_scalar_prefetch=2,
             grid=(steps,),
             in_specs=[whole, whole, whole, w_spec],
-            out_specs=(whole, whole),
+            out_specs=(whole, whole, whole),
             scratch_shapes=[
                 pltpu.VMEM((cells, 2 * LANES), BF16),
                 pltpu.VMEM((steps, slots, -(-classes // steps // LANES) * LANES), jnp.int32),
@@ -384,12 +410,9 @@
         cost_estimate=pl.CostEstimate(flops=20 * 10**9, bytes_accessed=50 * 10**6, transcendentals=0),
         name="to_source",
     )(me, source, multipoles, pair_first[0].T, pair_count, weights)
-    back = lax.all_to_all(returned, axes, 0, 0, tiled=True)
-
-    own, pair_first, pair_count = lax.optimization_barrier((own, pair_first, pair_count))
-    live = lax.broadcasted_iota(jnp.int32, (classes, slots), 1) < pair_count[0][:, None]
-    target_rows = jnp.where(live, pair_first[0], -1).reshape(steps, groups, GROUP)
-    place = (parent_of - position * parent_locals.shape[1] + HALO).reshape(1, cells)
+    back = exchange(returned)
+
+    target_rows = live.reshape(steps, groups, GROUP)
     base = pl.pallas_call(
         lambda *refs: target_kernel(devices, reach, slots, *refs[:14], refs[14:]),
         out_shape=jax.ShapeDtypeStruct((coeffs, cells), F32),
@@ -409,13 +432,14 @@
         compiler_params=pltpu.CompilerParams(vmem_limit_bytes=LIMIT),
         cost_estimate=pl.CostEstimate(flops=20 * 10**9, bytes_accessed=50 * 10**6, transcendentals=0),
         name="to_target",
-    )(me, source, multipoles, arrived, target_rows, weights, own, parents, place, octant.reshape(1, cells), l2l_ops)
+    )(me, source, multipoles, arrived, target_rows, weights, own, parents, parent_of.reshape(1, cells), octant.reshape(1, cells), l2l_ops)
 
     return pl.pallas_call(
         lambda me, *refs: back_kernel(devices, reach, me, *refs),
         out_shape=jax.ShapeDtypeStruct((coeffs, cells), F32),
-        in_specs=[smem(), vmem(), vmem(), vmem()],
+        in_specs=[smem(), vmem(), pl.BlockSpec(memory_space=pl.ANY), vmem()],
         out_specs=vmem(),
+        scratch_shapes=[pltpu.VMEM(back.shape, F32), pltpu.SemaphoreType.DMA],
         compiler_params=pltpu.CompilerParams(vmem_limit_bytes=LIMIT // 4),
         cost_estimate=pl.CostEstimate(flops=10**9, bytes_accessed=2 * 10**6, transcendentals=0),
         name="returned",

time: 91.4 us -> 87.8 us (0.961)
  other arithmetic: 1.87 us -> 0 us
  waiting for transfers between devices: 9.11 us -> 7.6 us
    all_to_all x2, waiting for transfers between devices: 9.11 us -> 7.6 us  [exchange(): return lax.all_to_all(cut, axes, 0, 0, tiled=True).reshape(blocks.shape)]
  transfers between devices with their start and end apart: 2 -> 2, of which waited for: 2 -> 2; matrix products, arithmetic and copies ran while one was open for 4% -> 2% of each run, Pallas kernels for 68% -> 71%
where the time goes in v4:
time: 87.8 us; the launch traced here: 87.3 us
  Pallas kernels  66.7 us (76%)
  starting transfers between devices  10.3 us (12%)
  waiting for transfers between devices  7.6 us (9%)
  local copies, waits for them, and re-layouts  2.47 us (3%)
    pallas_call x1, Pallas kernels, shards(): pl.pallas_call(lambda *refs: target_kernel(devices, reach, slots, *refs[:...  28.5 us
    pallas_call x1, Pallas kernels, shards(): pl.pallas_call(lambda me, src, x, t, n, w, r, o, v, table, lists, b0, b1,...  25 us
    all_to_all x2, starting transfers between devices, exchange(): return lax.all_to_all(cut, axes, 0, 0, tiled=True).reshape(blocks.shape)  10.3 us
    pallas_call x1, Pallas kernels, shards(): pl.pallas_call(ops_kernel, out_shape=jax.ShapeDtypeStruct((classes * rows...  8.11 us
    all_to_all x2, waiting for transfers between devices, exchange(): return lax.all_to_all(cut, axes, 0, 0, tiled=True).reshape(blocks.shape)  7.6 us
    pallas_call x1, Pallas kernels, shards(): pl.pallas_call(lambda me, *refs: export_kernel(me, devices, reach, *refs)...  2.99 us
    pallas_call x1, Pallas kernels, shards(): pl.pallas_call(lambda me, *refs: back_kernel(devices, reach, me, *refs),...  2.09 us
  transfers between devices with their start and end apart: 2, of which 2 were waited for; matrix products, arithmetic and copies ran while one was open for 2% of the time, Pallas kernels for 71%

profile of v4, /device:TPU:0, one launch (start us, length us, event | category | flops | bytes accessed | tf_op | source)
XLA Modules:
  0.0 87.3 jit_solution(7075587982658534864)
XLA Ops:
  0.0 3.0 %exports.1 = f32[2944,128]{1,0:T(8,128)} custom-call(s32[1]{0:T(128)} %bitcast.me.refs_0_, f32[81,512]{1,0:T(8,128)} %refs_2_.1, s32[26,1,128]{2,1,0:T(1,128)} %bitcast.16, f32[64,81]{1,0:T(8,128)} %bitcast.24), custom_call_target="tpu_custom_call" | custom-call | flops 1000000000 | bytes 2000000 | tf_op jit(solution)/shard_map/exports/pallas_call | solution.py:361
  3.0 7.3 %all-to-all-start = ((f32[32,92,1,128]{3,2,1,0:T(1,128)}), f32[32,92,1,128]{3,2,1,0:T(1,128)S(1)}, u32[]{:S(2)}, u32[]{:S(2)}) async-start(f32[32,92,1,128]{3,2,1,0:T(1,128)} %bitcast.19), calls=%async_computation | async-start | bytes 3014656 | tf_op jit(solution)/shard_map/all_to_all | solution.py:359
  10.3 8.1 %operators.1.w.refs_5_ = f32[22528,128]{1,0:T(8,128)} custom-call(f32[81,81,256]{2,1,0:T(8,128)} %m2l_ref.1), custom_call_target="tpu_custom_call" | custom-call | flops 1000000000 | bytes 20000000 | tf_op jit(solution)/shard_map/operators/pallas_call | solution.py:372
  18.4 25.0 %to_source.1 = (f32[2592,128]{1,0:T(8,128)}, f32[512,128]{1,0:T(8,128)}, s32[256,64]{1,0:T(8,128)}) custom-call(s32[1]{0:T(128)} %bitcast.me.refs_0_, s32[64,256]{1,0:T(8,128)} %bitcast.22, f32[81,512]{1,0:T(8,128)} %refs_2_.1, s32[64,256]{1,0:T(8,128)} %bitcast.21, s32[1,256]{1,0:T(1,128)} %n.1, f32[22528,128]{1,0:T(8,128)} %operators.1.w.refs_5_), custom_call_target="tpu_custom_call" | custom-call | flops 20000000000 | bytes 50000000 | tf_op jit(solution)/shard_map/to_source/pallas_call | solution.py:387
  43.4 0.0 copy-start.3
  43.4 4.3 %all-to-all-done = f32[32,92,1,128]{3,2,1,0:T(1,128)S(1)} async-done(((f32[32,92,1,128]{3,2,1,0:T(1,128)}), f32[32,92,1,128]{3,2,1,0:T(1,128)S(1)}, u32[]{:S(2)}, u32[]{:S(2)}) %all-to-all-start) | async-done | bytes 1507360 | tf_op jit(solution)/shard_map/all_to_all | solution.py:359
  47.7 0.0 copy-start.2
  47.7 0.0 copy-start.4
  47.7 3.0 %all-to-all-start.1 = ((f32[32,81,1,128]{3,2,1,0:T(1,128)}), f32[32,81,1,128]{3,2,1,0:T(1,128)S(1)}, u32[]{:S(2)}, u32[]{:S(2)}) async-start(f32[32,81,1,128]{3,2,1,0:T(1,128)} %bitcast.20), calls=%async_computation.1 | async-start | bytes 2654208 | tf_op jit(solution)/shard_map/all_to_all | solution.py:359
  50.7 0.0 copy-done.3
  50.7 0.8 copy.14.refs_10_
  51.5 0.0 copy-done.2
  51.5 0.0 copy-done.4
  51.5 0.7 reshape.27.refs_4_
  52.3 0.0 copy-start
  52.3 28.5 %to_target.1.refs_0_ = f32[81,512]{1,0:T(8,128)} custom-call(s32[1]{0:T(128)} %bitcast.me.refs_0_, s32[64,256]{1,0:T(8,128)} %bitcast.23, f32[81,512]{1,0:T(8,128)} %refs_2_.1, f32[2944,128]{1,0:T(8,128)} %bitcast.18, s32[4,16,256]{2,1,0:T(8,128)} %reshape.27.refs_4_, f32[22528,128]{1,0:T(8,128)} %operators.1.w.refs_5_, ...), custom_call_target="tpu_custom_call" | custom-call | flops 20000000000 | bytes 50000000 | tf_op jit(solution)/shard_map/to_target/pallas_call | solution.py:416
  80.8 3.3 %all-to-all-done.1 = f32[32,81,1,128]{3,2,1,0:T(1,128)S(1)} async-done(((f32[32,81,1,128]{3,2,1,0:T(1,128)}), f32[32,81,1,128]{3,2,1,0:T(1,128)S(1)}, u32[]{:S(2)}, u32[]{:S(2)}) %all-to-all-start.1) | async-done | bytes 1327136 | tf_op jit(solution)/shard_map/all_to_all | solution.py:359
  84.1 0.0 copy-done
  84.1 0.0 copy-start.1
  84.1 0.9 %copy-done.1 = f32[81,512]{1,0:T(8,128)S(1)} copy-done((f32[81,512]{1,0:T(8,128)S(1)}, f32[81,512]{1,0:T(8,128)}, u32[]{:S(2)}) %copy-start.1) | copy-done | bytes 165912
  85.0 2.1 %returned.1 = f32[81,512]{1,0:T(8,128)} custom-call(s32[1]{0:T(128)} %bitcast.me.refs_0_, f32[81,512]{1,0:T(8,128)S(1)} %copy-done.1, f32[2592,128]{1,0:T(8,128)S(1)} %bitcast.15, s32[26,1,128]{2,1,0:T(1,128)S(1)} %bitcast.17), custom_call_target="tpu_custom_call" | custom-call | flops 1000000000 | bytes 2000000 | tf_op jit(solution)/shard_map/returned/pallas_call | solution.py:437
Async XLA Ops:
  3.0 44.7 %all-to-all-start = ((f32[32,92,1,128]{3,2,1,0:T(1,128)}), f32[32,92,1,128]{3,2,1,0:T(1,128)S(1)}, u32[]{:S(2)}, u32[]{:S(2)}) async-start(f32[32,92,1,128]{3,2,1,0:T(1,128)} %bitcast.19), calls=%async_computation | async-start | bytes 3014656 | tf_op jit(solution)/shard_map/all_to_all | solution.py:359
  43.4 7.3 %copy-start.3 = (f32[8,81,81]{2,0,1:T(8,128)S(1)}, f32[8,81,81]{2,0,1:T(8,128)}, u32[]{:S(2)}) copy-start(f32[8,81,81]{2,0,1:T(8,128)} %param.13) | copy-start | bytes 629860
  47.7 3.8 %copy-start.2 = (f32[32,92,1,128]{3,2,1,0:T(1,128)}, f32[32,92,1,128]{3,2,1,0:T(1,128)S(1)}, u32[]{:S(2)}) copy-start(f32[32,92,1,128]{3,2,1,0:T(1,128)S(1)} %all-to-all-done) | copy-start | bytes 4521988
  47.7 3.8 %copy-start.4 = (s32[256,64]{1,0:T(8,128)S(1)}, s32[256,64]{1,0:T(8,128)}, u32[]{:S(2)}) copy-start(s32[256,64]{1,0:T(8,128)} %get-tuple-element.8) | copy-start | bytes 196612
  47.7 36.4 %all-to-all-start.1 = ((f32[32,81,1,128]{3,2,1,0:T(1,128)}), f32[32,81,1,128]{3,2,1,0:T(1,128)S(1)}, u32[]{:S(2)}, u32[]{:S(2)}) async-start(f32[32,81,1,128]{3,2,1,0:T(1,128)} %bitcast.20), calls=%async_computation.1 | async-start | bytes 2654208 | tf_op jit(solution)/shard_map/all_to_all | solution.py:359
  52.3 31.8 %copy-start = (s32[1,26,128]{2,0,1:T(1,128)S(1)}, s32[1,26,128]{2,0,1:T(1,128)}, u32[]{:S(2)}) copy-start(s32[1,26,128]{2,0,1:T(1,128)} %param.14) | copy-start | bytes 39940
  84.1 0.9 %copy-start.1 = (f32[81,512]{1,0:T(8,128)S(1)}, f32[81,512]{1,0:T(8,128)}, u32[]{:S(2)}) copy-start(f32[81,512]{1,0:T(8,128)} %to_target.1.refs_0_) | copy-start | bytes 497668

commit v5 on v4

--- a/solution.py
+++ b/solution.py
@@ -136,18 +136,18 @@
         out_ref[pl.ds(other * held + coeffs, held - coeffs), :] = halo_out(parents, coeffs)
 
 
-def ops_kernel(m2l_ref, out_ref, turned):
+def lay_out(m2l_ref, half, w_ref, turned):
     coeffs = m2l_ref.shape[0]
-    pitch = out_ref.shape[0] // LANES
+    pitch = w_ref.shape[1] // LANES
     for i in range(coeffs):
         turned[pl.ds(i, pitch, pitch), :] = pad_rows(m2l_ref[i], pitch)
     for j in range(coeffs):
         block = pad_rows(turned[j * pitch : j * pitch + coeffs, :], LANES).T
-        out_ref[pl.ds(j, LANES, pitch), :] = block
-    out_ref[pl.ds(coeffs, LANES, pitch), :] = block
-    out_ref[pl.ds(coeffs + 1, LANES, pitch), :] = block - block.astype(BF16).astype(F32)
+        w_ref[half, pl.ds(j, LANES, pitch), :] = block
+    w_ref[half, pl.ds(coeffs, LANES, pitch), :] = block
+    w_ref[half, pl.ds(coeffs + 1, LANES, pitch), :] = block - block.astype(BF16).astype(F32)
     for j in range(coeffs + 2, pitch):
-        out_ref[pl.ds(j, LANES, pitch), :] = jnp.zeros((LANES, LANES), F32)
+        w_ref[half, pl.ds(j, LANES, pitch), :] = jnp.zeros((LANES, LANES), F32)
 
 
 def weights_of(w_ref, start, pitch, coeffs):
@@ -170,7 +170,10 @@
     )
 
 
-def source_kernel(devices, reach, steps_total, me, src, x_ref, tgt_ref, cnt_ref, w_ref, ret_ref, own_ref, live_ref, table, lists, bufs, accs):
+def source_kernel(
+    devices, reach, steps_total, me, src, x_ref, tgt_ref, cnt_ref, m2l_ref, ret_ref, own_ref, live_ref, w_any,
+    table, lists, w_all, turned, sent, bufs, accs,
+):
     step = pl.program_id(0)
     steps = pl.num_programs(0)
     coeffs, cells = x_ref.shape
@@ -178,7 +181,21 @@
     block = classes // steps
     per = GROUP // slots
     groups = block // per
-    pitch = w_ref.shape[0] // block
+    pitch = w_all.shape[1] // LANES
+    halves = w_all.shape[0]
+    span = steps_total // halves
+    half = step // span
+
+    def copy_of(k):
+        return pltpu.make_async_copy(w_all.at[k], w_any.at[k], sent.at[k])
+
+    @pl.when(step % span == 0)
+    def _():
+        lay_out(m2l_ref, half, w_all, turned)
+        copy_of(half).start()
+
+    first = pl.multiple_of((step % span) * block * pitch, 8)
+    w_ref = w_all.at[half, pl.ds(first, block * pitch), :]
 
     @pl.when(step == 0)
     def _():
@@ -221,6 +238,8 @@
 
     @pl.when(step == steps - 1)
     def _():
+        for k in range(halves):
+            copy_of(k).wait()
         sign = parity_at(lax.broadcasted_iota(jnp.int32, (LANES, LANES), 1))
 
         def total(start):
@@ -302,14 +321,11 @@
         out_ref[...] = total
 
 
-def back_kernel(devices, reach, me, base_ref, got_any, idx_ref, out_ref, got_ref, done):
+def back_kernel(devices, reach, me, base_ref, got_ref, idx_ref, out_ref):
     coeffs, cells = base_ref.shape
     rows = -(-coeffs // 8) * 8
-    copy = pltpu.make_async_copy(got_any, got_ref, done)
-    copy.start()
     line = lax.broadcasted_iota(jnp.int32, (cells, LANES), 0)
     total = jnp.zeros((2 * rows, cells), F32)
-    copy.wait()
     for slot in range(0, idx_ref.shape[0], 2):
         hots, gots = [], []
         for k in (slot, slot + 1):
@@ -360,7 +376,7 @@
 
     outgoing = pl.pallas_call(
         lambda me, *refs: export_kernel(me, devices, reach, *refs),
-        out_shape=jax.ShapeDtypeStruct((devices * held, send), F32),
+        out_shape=pltpu.VMEM((devices * held, send), F32),
         in_specs=[smem(), vmem(), vmem(), vmem()],
         out_specs=vmem(),
         compiler_params=pltpu.CompilerParams(vmem_limit_bytes=LIMIT),
@@ -369,38 +385,32 @@
     )(me, multipoles, exported, parents)
     arrived = exchange(outgoing)
 
-    weights = pl.pallas_call(
-        ops_kernel,
-        out_shape=jax.ShapeDtypeStruct((classes * rows, LANES), F32),
-        grid=(classes // LANES,),
-        in_specs=[pl.BlockSpec((coeffs, coeffs, LANES), lambda s: (0, 0, s))],
-        out_specs=pl.BlockSpec((LANES * rows, LANES), lambda s: (s, 0)),
-        scratch_shapes=[pltpu.VMEM((rows * rows, LANES), F32)],
-        compiler_params=pltpu.CompilerParams(vmem_limit_bytes=LIMIT),
-        cost_estimate=pl.CostEstimate(flops=10**9, bytes_accessed=20 * 10**6, transcendentals=0),
-        name="operators",
-    )(m2l_ops)
-
     source = pair_second[0].T
     w_spec = pl.BlockSpec((groups * GROUP // slots * rows, LANES), lambda s, *_: (s, 0))
     whole = pl.BlockSpec(memory_space=pltpu.VMEM)
-    returned, own, live = pl.pallas_call(
-        lambda me, src, x, t, n, w, r, o, v, table, lists, b0, b1, *accs: source_kernel(
-            devices, reach, steps, me, src, x, t, n, w, r, o, v, table, lists, (b0, b1), accs
+    halves = classes // LANES
+    span = steps // halves
+    returned, own, live, weights = pl.pallas_call(
+        lambda me, src, x, t, n, m, r, o, v, w, table, lists, wa, turned, sent, b0, b1, *accs: source_kernel(
+            devices, reach, steps, me, src, x, t, n, m, r, o, v, w, table, lists, wa, turned, sent, (b0, b1), accs
         ),
         out_shape=(
             jax.ShapeDtypeStruct((devices * coeffs, send), F32),
             jax.ShapeDtypeStruct((cells, LANES), F32),
             jax.ShapeDtypeStruct((classes, slots), jnp.int32),
+            jax.ShapeDtypeStruct((halves, LANES * rows, LANES), F32),
         ),
         grid_spec=pltpu.PrefetchScalarGridSpec(
             num_scalar_prefetch=2,
             grid=(steps,),
-            in_specs=[whole, whole, whole, w_spec],
-            out_specs=(whole, whole, whole),
+            in_specs=[whole, whole, whole, pl.BlockSpec((coeffs, coeffs, LANES), lambda s, *_: (0, 0, s // span))],
+            out_specs=(whole, whole, whole, pl.BlockSpec(memory_space=pl.ANY)),
             scratch_shapes=[
                 pltpu.VMEM((cells, 2 * LANES), BF16),
                 pltpu.VMEM((steps, slots, -(-classes // steps // LANES) * LANES), jnp.int32),
+                pltpu.VMEM((halves, LANES * rows, LANES), F32),
+                pltpu.VMEM((rows * rows, LANES), F32),
+                pltpu.SemaphoreType.DMA((halves,)),
                 pltpu.VMEM((GROUP, LANES), F32),
                 pltpu.VMEM((GROUP, LANES), F32),
             ]
@@ -409,13 +419,14 @@
         compiler_params=pltpu.CompilerParams(vmem_limit_bytes=LIMIT),
         cost_estimate=pl.CostEstimate(flops=20 * 10**9, bytes_accessed=50 * 10**6, transcendentals=0),
         name="to_source",
-    )(me, source, multipoles, pair_first[0].T, pair_count, weights)
-    back = exchange(returned)
+    )(me, source, multipoles, pair_first[0].T, pair_count, m2l_ops)
+    weights = weights.reshape(classes * rows, LANES)
+    back = pltpu.with_memory_space_constraint(exchange(returned), pltpu.VMEM)
 
     target_rows = live.reshape(steps, groups, GROUP)
     base = pl.pallas_call(
         lambda *refs: target_kernel(devices, reach, slots, *refs[:14], refs[14:]),
-        out_shape=jax.ShapeDtypeStruct((coeffs, cells), F32),
+        out_shape=pltpu.VMEM((coeffs, cells), F32),
         grid_spec=pltpu.PrefetchScalarGridSpec(
             num_scalar_prefetch=2,
             grid=(steps,),
@@ -437,9 +448,8 @@
     return pl.pallas_call(
         lambda me, *refs: back_kernel(devices, reach, me, *refs),
         out_shape=jax.ShapeDtypeStruct((coeffs, cells), F32),
-        in_specs=[smem(), vmem(), pl.BlockSpec(memory_space=pl.ANY), vmem()],
+        in_specs=[smem(), vmem(), vmem(), vmem()],
         out_specs=vmem(),
-        scratch_shapes=[pltpu.VMEM(back.shape, F32), pltpu.SemaphoreType.DMA],
         compiler_params=pltpu.CompilerParams(vmem_limit_bytes=LIMIT // 4),
         cost_estimate=pl.CostEstimate(flops=10**9, bytes_accessed=2 * 10**6, transcendentals=0),
         name="returned",

time: 87.8 us -> 86.5 us (0.985)
  Pallas kernels: 66.7 us -> 61.6 us
  waiting for transfers between devices: 7.6 us -> 12.6 us
  local copies, waits for them, and re-layouts: 2.47 us -> 1.55 us
    all_to_all x2, waiting for transfers between devices: 7.6 us -> 12.6 us  [exchange(): return lax.all_to_all(cut, axes, 0, 0, tiled=True).reshape(blocks.shape)]
    pallas_call x2 -> x1, Pallas kernels: 33.1 us -> 28.7 us  [shards(): pl.pallas_call(lambda me, src, x, t, n, m, r, o, v, w, table, lists, wa,...]
    unnamed x11 -> x9, local copies, waits for them, and re-layouts: 1.75 us -> 0.82 us
  transfers between devices with their start and end apart: 2 -> 2, of which waited for: 2 -> 2; matrix products, arithmetic and copies ran while one was open for 2% -> 2% of each run, Pallas kernels for 71% -> 66%
where the time goes in v5:
time: 86.5 us; the launch traced here: 86.1 us
  Pallas kernels  61.6 us (71%)
  waiting for transfers between devices  12.6 us (15%)
  starting transfers between devices  10.3 us (12%)
  local copies, waits for them, and re-layouts  1.55 us (2%)
    pallas_call x1, Pallas kernels, shards(): pl.pallas_call(lambda me, src, x, t, n, m, r, o, v, w, table, lists, wa,...  28.7 us
    pallas_call x1, Pallas kernels, shards(): pl.pallas_call(lambda *refs: target_kernel(devices, reach, slots, *refs[:...  27.9 us
    all_to_all x2, waiting for transfers between devices, exchange(): return lax.all_to_all(cut, axes, 0, 0, tiled=True).reshape(blocks.shape)  12.6 us
    all_to_all x2, starting transfers between devices, exchange(): return lax.all_to_all(cut, axes, 0, 0, tiled=True).reshape(blocks.shape)  10.3 us
    pallas_call x1, Pallas kernels, shards(): pl.pallas_call(lambda me, *refs: export_kernel(me, devices, reach, *refs)...  2.99 us
    pallas_call x1, Pallas kernels, shards(): pl.pallas_call(lambda me, *refs: back_kernel(devices, reach, me, *refs),...  1.97 us
  transfers between devices with their start and end apart: 2, of which 2 were waited for; matrix products, arithmetic and copies ran while one was open for 2% of the time, Pallas kernels for 66%

profile of v5, /device:TPU:0, one launch (start us, length us, event | category | flops | bytes accessed | tf_op | source)
XLA Modules:
  0.0 86.1 jit_solution(5125790287333155263)
XLA Ops:
  0.0 3.0 %exports.1 = f32[2944,128]{1,0:T(8,128)} custom-call(s32[1]{0:T(128)} %bitcast.me.refs_0_, f32[81,512]{1,0:T(8,128)} %refs_2_.1, s32[26,1,128]{2,1,0:T(1,128)} %bitcast.17, f32[64,81]{1,0:T(8,128)} %bitcast.24), custom_call_target="tpu_custom_call" | custom-call | flops 1000000000 | bytes 2000000 | tf_op jit(solution)/shard_map/exports/pallas_call | solution.py:377
  3.0 7.3 %all-to-all-start = ((f32[32,92,1,128]{3,2,1,0:T(1,128)}), f32[32,92,1,128]{3,2,1,0:T(1,128)S(1)}, u32[]{:S(2)}, u32[]{:S(2)}) async-start(f32[32,92,1,128]{3,2,1,0:T(1,128)} %bitcast.5), calls=%async_computation | async-start | bytes 3014656 | tf_op jit(solution)/shard_map/all_to_all | solution.py:375
  10.3 28.7 %to_source.1 = (f32[2592,128]{1,0:T(8,128)}, f32[512,128]{1,0:T(8,128)}, s32[256,64]{1,0:T(8,128)}, f32[2,11264,128]{2,1,0:T(8,128)}) custom-call(s32[1]{0:T(128)} %bitcast.me.refs_0_, s32[64,256]{1,0:T(8,128)} %bitcast.22, f32[81,512]{1,0:T(8,128)} %refs_2_.1, s32[64,256]{1,0:T(8,128)} %bitcast.21, s32[1,256]{1,0:T(1,128)} %n.1, f32[81,81,256]{2,1,0:T(8,128)} %m.1), custom_call_target="tpu_custom_call" | custom-call | flops 20000000000 | bytes 50000000 | tf_op jit(solution)/shard_map/to_source/pallas_call | solution.py:393
  39.0 0.0 copy-start.2
  39.0 8.7 %all-to-all-done = f32[32,92,1,128]{3,2,1,0:T(1,128)S(1)} async-done(((f32[32,92,1,128]{3,2,1,0:T(1,128)}), f32[32,92,1,128]{3,2,1,0:T(1,128)S(1)}, u32[]{:S(2)}, u32[]{:S(2)}) %all-to-all-start) | async-done | bytes 1507360 | tf_op jit(solution)/shard_map/all_to_all | solution.py:375
  47.7 0.0 copy-start.1
  47.7 0.0 copy-start.3
  47.7 3.0 %all-to-all-start.1 = ((f32[32,81,1,128]{3,2,1,0:T(1,128)}), f32[32,81,1,128]{3,2,1,0:T(1,128)S(1)}, u32[]{:S(2)}, u32[]{:S(2)}) async-start(f32[32,81,1,128]{3,2,1,0:T(1,128)} %bitcast.20), calls=%async_computation.1 | async-start | bytes 2654208 | tf_op jit(solution)/shard_map/all_to_all | solution.py:375
  50.7 0.0 copy-done.2
  50.7 0.8 copy.14.refs_10_
  51.5 0.0 copy-done.1
  51.5 0.0 copy-done.3
  51.5 0.7 reshape.30.refs_4_
  52.3 0.0 copy-start
  52.3 27.9 %to_target.1.refs_0_ = f32[81,512]{1,0:T(8,128)S(1)} custom-call(s32[1]{0:T(128)} %bitcast.me.refs_0_, s32[64,256]{1,0:T(8,128)} %bitcast.23, f32[81,512]{1,0:T(8,128)} %refs_2_.1, f32[2944,128]{1,0:T(8,128)} %bitcast.19, s32[4,16,256]{2,1,0:T(8,128)} %reshape.30.refs_4_, f32[22528,128]{1,0:T(8,128)} %bitcast.28, f32[512,128]{1,0:T(8,128)} %get-tuple-element.11.refs_6_, ...), custom_call_target="tpu_custom_call" | custom-call | flops 20000000000 | bytes 50000000 | tf_op jit(solution)/shard_map/to_target/pallas_call | solution.py:427
  80.2 3.9 %all-to-all-done.1 = f32[32,81,1,128]{3,2,1,0:T(1,128)S(1)} async-done(((f32[32,81,1,128]{3,2,1,0:T(1,128)}), f32[32,81,1,128]{3,2,1,0:T(1,128)S(1)}, u32[]{:S(2)}, u32[]{:S(2)}) %all-to-all-start.1) | async-done | bytes 1327136 | tf_op jit(solution)/shard_map/all_to_all | solution.py:375
  84.1 0.0 copy-done
  84.1 2.0 %returned.1 = f32[81,512]{1,0:T(8,128)} custom-call(s32[1]{0:T(128)} %bitcast.me.refs_0_, f32[81,512]{1,0:T(8,128)S(1)} %to_target.1.refs_0_, f32[2592,128]{1,0:T(8,128)S(1)} %bitcast.16, s32[26,1,128]{2,1,0:T(1,128)S(1)} %bitcast.18), custom_call_target="tpu_custom_call" | custom-call | flops 1000000000 | bytes 2000000 | tf_op jit(solution)/shard_map/returned/pallas_call | solution.py:448
Async XLA Ops:
  3.0 44.7 %all-to-all-start = ((f32[32,92,1,128]{3,2,1,0:T(1,128)}), f32[32,92,1,128]{3,2,1,0:T(1,128)S(1)}, u32[]{:S(2)}, u32[]{:S(2)}) async-start(f32[32,92,1,128]{3,2,1,0:T(1,128)} %bitcast.5), calls=%async_computation | async-start | bytes 3014656 | tf_op jit(solution)/shard_map/all_to_all | solution.py:375
  39.0 11.7 %copy-start.2 = (f32[8,81,81]{2,0,1:T(8,128)S(1)}, f32[8,81,81]{2,0,1:T(8,128)}, u32[]{:S(2)}) copy-start(f32[8,81,81]{2,0,1:T(8,128)} %param.13) | copy-start | bytes 629860
  47.7 3.8 %copy-start.1 = (f32[32,92,1,128]{3,2,1,0:T(1,128)}, f32[32,92,1,128]{3,2,1,0:T(1,128)S(1)}, u32[]{:S(2)}) copy-start(f32[32,92,1,128]{3,2,1,0:T(1,128)S(1)} %all-to-all-done) | copy-start | bytes 4521988
  47.7 3.8 %copy-start.3 = (s32[256,64]{1,0:T(8,128)S(1)}, s32[256,64]{1,0:T(8,128)}, u32[]{:S(2)}) copy-start(s32[256,64]{1,0:T(8,128)} %get-tuple-element.9) | copy-start | bytes 196612
  47.7 36.4 %all-to-all-start.1 = ((f32[32,81,1,128]{3,2,1,0:T(1,128)}), f32[32,81,1,128]{3,2,1,0:T(1,128)S(1)}, u32[]{:S(2)}, u32[]{:S(2)}) async-start(f32[32,81,1,128]{3,2,1,0:T(1,128)} %bitcast.20), calls=%async_computation.1 | async-start | bytes 2654208 | tf_op jit(solution)/shard_map/all_to_all | solution.py:375
  52.3 31.8 %copy-start = (s32[1,26,128]{2,0,1:T(1,128)S(1)}, s32[1,26,128]{2,0,1:T(1,128)}, u32[]{:S(2)}) copy-start(s32[1,26,128]{2,0,1:T(1,128)} %param.14) | copy-start | bytes 39940
